TPU v7x, 32 devices: a whole 2x2x4 slice. The times are simulated.
32 devices in a mesh: row: 2 (over x), col: 16 (over z, y, core).
Axes of the slice: x: 2, y: 2, z: 4, core: 2. Of those that a mesh axis runs over, the one named last changes fastest.
Arguments:
- matrix: float32 [16384, 16384], P('row', 'col'), may hold values from -6 to 6, as said below
- vectors: float32 [2, 16384, 128], P(None, ('row', 'col')), may hold values from -0.16 to 0.16
- tfactor: float32 [2, 128, 128], replicated, may hold values from -0.5 to 0.5
Outputs:
- updated: float32 [16384, 16384], P('row', 'col')
Inputs may be any that keep to these rules, and one draw needn't show every extreme that they name: matrix is symmetric: matrix[i, j] equals matrix[j, i].
All inputs are finite; a program needn't handle non-finite values.
Results may differ from a plain program's by a relative error of at most 0.00012.
Values sent between devices are 32-bit elements; how exact they have to be, the bound alone decides.
No kernel may reach another device: no remote copies, remote signals or barrier semaphores. Data moves between devices by JAX's collectives and lax.ppermute only.
A program may use at most 192 MiB of HBM per device.

v0:
```python
import jax
import jax.numpy as jnp
from jax import lax
from jax.sharding import PartitionSpec as P

highest = lax.Precision.HIGHEST


def spread(block, axis, source):
    block = jnp.where(lax.axis_index(axis) == source, block, jnp.zeros_like(block))
    return lax.psum(block, axis)


def mat_product(left, right):
    return jnp.dot(left, right, precision=highest, preferred_element_type=jnp.float32)


def body(matrix, vectors, tfactor):
    rows_here, cols_here = matrix.shape
    panels = vectors.shape[0]
    own_count = vectors.shape[1]
    row_total = lax.axis_size("row")
    col_total = lax.axis_size("col")
    col_index = lax.axis_index("col")
    owner_row = col_index * row_total // col_total
    offset = col_index * cols_here - owner_row * rows_here
    v_rows = lax.all_gather(vectors, "col", axis=1, tiled=True)
    v_local = lax.dynamic_slice_in_dim(v_rows, offset, cols_here, 1)
    v_cols = spread(v_local, "row", owner_row)
    current = matrix
    for panel_index in range(panels):
        vector_i = v_rows[panel_index]
        vector_j = v_cols[panel_index]
        own_rows = vectors[panel_index]
        factor = jnp.triu(tfactor[panel_index])

        def partial_rows(begin_row, span_rows, current=current, vector_j=vector_j):
            return mat_product(current, vector_j)

        summed = lax.psum_scatter(
            partial_rows(jnp.int32(0), own_count * lax.axis_size("col")),
            "col",
            scatter_dimension=0,
            tiled=True,
        )
        ymatrix = mat_product(summed, factor)
        gram_matrix = lax.psum(mat_product(own_rows.T, ymatrix), ("row", "col"))
        w_own = ymatrix - 0.5 * mat_product(own_rows, mat_product(factor.T, gram_matrix))
        w_i = lax.all_gather(w_own, "col", axis=0, tiled=True)
        w_j = spread(lax.dynamic_slice_in_dim(w_i, offset, cols_here, 0), "row", owner_row)
        current = current - mat_product(vector_i, w_j.T) - mat_product(w_i, vector_j.T)
    return current


def solution(mesh):
    return jax.shard_map(
        body,
        mesh=mesh,
        in_specs=(P("row", "col"), P(None, ("row", "col"), None), P()),
        out_specs=P("row", "col"),
        check_vma=False,
    )
```

profile of v0, /device:TPU:0, one launch (start us, length us, event | category | flops | bytes accessed | tf_op | source)
XLA Modules:
  0.0 926.7 jit_solution(3131454637471280595)
XLA Ops:
  6.5 0.0 all-gather.4.cloned.1.call-start
  6.5 0.7 all-gather.4.cloned.1.call-update
  7.3 0.0 all-reduce.6.cloned.1.call-start
  7.3 79.9 %all-gather.4.cloned.1.call-done = f32[2,8192,128]{2,1,0:T(8,128)} async-done(((f32[2,512,128]{2,1,0:T(8,128)}), f32[2,8192,128]{2,1,0:T(8,128)}) %all-gather.4.cloned.1.call-update) | async-done | bytes 8388624 | tf_op jit(solution)/shard_map/all_gather | solution.py:27
  87.2 2.3 dynamic-slice_select_fusion
  89.5 0.0 all-reduce.6.cloned.1.call-update
  89.5 0.0 reduce-scatter.3.cloned.1.call-start
  89.5 38.4 %all-reduce.6.cloned.1.call-done = f32[2,1024,128]{2,1,0:T(8,128)} async-done(((f32[2,1024,128]{2,1,0:T(8,128)}), f32[2,1024,128]{2,1,0:T(8,128)}) %all-reduce.6.cloned.1.call-update) | async-done | bytes 1048592 | tf_op jit(solution)/shard_map/psum | solution.py:11
  127.9 39.6 %convolution_bitcast_fusion = f32[8192,128]{0,1:T(8,128)} fusion(f32[8192,1024]{1,0:T(8,128)} %param.3, f32[2,1024,128]{2,1,0:T(8,128)} %all-reduce.6.cloned.1.call-done), kind=kOutput, calls=%fused_computation.4 | convolution fusion | flops 12884901888 | bytes 38273024 | tf_op jit(solution)/shard_map/dot_general | solution.py:15
  167.6 0.0 reduce-scatter.3.cloned.1.call-update
  167.6 0.0 all-reduce.8.cloned.1.call-start
  167.7 72.5 %reduce-scatter.3.cloned.1.call-done = f32[512,128]{0,1:T(8,128)} async-done(((f32[8192,128]{0,1:T(8,128)}), f32[512,128]{0,1:T(8,128)}) %reduce-scatter.3.cloned.1.call-update) | async-done | bytes 262160 | tf_op jit(solution)/shard_map/reduce_scatter | solution.py:40
  240.2 0.0 copy-done.2
  240.2 1.6 fusion.18
  241.7 1.2 convolution_bitcast_fusion.2
  243.0 0.0 all-reduce.8.cloned.1.call-update
  243.0 0.0 all-gather.6.cloned.1.call-start
  243.0 119.2 %all-reduce.8.cloned.1.call-done = f32[128,128]{0,1:T(8,128)} async-done(((f32[128,128]{0,1:T(8,128)}), f32[128,128]{0,1:T(8,128)}) %all-reduce.8.cloned.1.call-update) | async-done | bytes 65552 | tf_op jit(solution)/shard_map/psum | solution.py:47
  362.2 1.2 fusion.17
  363.4 1.1 fusion.5
  364.5 0.0 all-gather.6.cloned.1.call-update
  364.5 0.0 all-reduce.10.cloned.1.call-start
  364.6 31.2 %copy.5 = f32[8192,1024]{0,1:T(8,128)} copy(f32[8192,1024]{1,0:T(8,128)} %param.3) | data formatting | bytes 67108864 | tf_op args[0]
  395.7 20.3 %all-gather.6.cloned.1.call-done = f32[8192,128]{1,0:T(8,128)} async-done(((f32[512,128]{1,0:T(8,128)}), f32[8192,128]{1,0:T(8,128)}) %all-gather.6.cloned.1.call-update) | async-done | bytes 4194320 | tf_op jit(solution)/shard_map/all_gather | solution.py:49
  416.0 1.9 dynamic-slice_select_fusion.2
  417.9 0.0 all-reduce.10.cloned.1.call-update
  417.9 0.3 reduce-scatter.5.cloned.1.call-start
  418.2 31.4 %fusion.6 = f32[8192,1024]{0,1:T(8,128)} fusion(f32[8192,128]{1,0:T(8,128)} %all-gather.6.cloned.1.call-done, f32[2,1024,128]{2,1,0:T(8,128)S(1)} %copy-done), kind=kOutput, calls=%fused_computation.20 | convolution fusion | flops 12884901888 | bytes 38273024 | tf_op jit(solution)/shard_map/dot_general | solution.py:15
  449.7 44.7 %fusion.1 = f32[8192,1024]{0,1:T(8,128)} fusion(f32[8192,1024]{0,1:T(8,128)} %fusion.6, f32[8192,1024]{0,1:T(8,128)} %copy.5, f32[1024,128]{1,0:T(8,128)} %all-reduce.10.cloned.1.call-done, f32[2,8192,128]{2,1,0:T(8,128)} %all-gather.4.cloned.1.call-done), kind=kOutput, calls=%fused_computation.3 | convolution fusion | flops 12901679104 | bytes 105381888 | tf_op jit(solution)/shard_map/dot_general | solution.py:15
  494.3 66.7 %fusion.8 = f32[8192,128]{1,0:T(8,128)} fusion(f32[8192,1024]{0,1:T(8,128)} %fusion.1, f32[2,1024,128]{2,1,0:T(8,128)S(1)} %copy-done), kind=kOutput, calls=%fused_computation.22 | convolution fusion | flops 12884901888 | bytes 38273024 | tf_op jit(solution)/shard_map/dot_general | solution.py:15
  561.1 0.0 reduce-scatter.5.cloned.1.call-update
  561.1 0.0 all-reduce.12.cloned.1.call-start
  561.2 71.0 %reduce-scatter.5.cloned.1.call-done = f32[512,128]{1,0:T(8,128)} async-done(((f32[8192,128]{1,0:T(8,128)}), f32[512,128]{1,0:T(8,128)}) %reduce-scatter.5.cloned.1.call-update) | async-done | bytes 262160 | tf_op jit(solution)/shard_map/reduce_scatter | solution.py:40
  632.2 1.4 fusion.20
  633.6 1.2 convolution_bitcast_fusion.1
  634.8 0.0 all-reduce.12.cloned.1.call-update
  634.8 0.0 all-gather.8.cloned.1.call-start
  634.9 119.4 %all-reduce.12.cloned.1.call-done = f32[128,128]{0,1:T(8,128)} async-done(((f32[128,128]{0,1:T(8,128)}), f32[128,128]{0,1:T(8,128)}) %all-reduce.12.cloned.1.call-update) | async-done | bytes 65552 | tf_op jit(solution)/shard_map/psum | solution.py:47
  754.3 1.2 fusion.19
  755.5 1.1 fusion.3
  756.6 0.0 all-gather.8.cloned.1.call-update
  756.6 0.0 all-reduce.14.cloned.1.call-start
  756.7 51.5 %all-gather.8.cloned.1.call-done = f32[8192,128]{1,0:T(8,128)} async-done(((f32[512,128]{1,0:T(8,128)}), f32[8192,128]{1,0:T(8,128)}) %all-gather.8.cloned.1.call-update) | async-done | bytes 4194320 | tf_op jit(solution)/shard_map/all_gather | solution.py:49
  808.1 1.9 dynamic-slice_select_fusion.1
  810.0 0.0 all-reduce.14.cloned.1.call-update
  810.0 31.2 %fusion.7 = f32[8192,1024]{0,1:T(8,128)} fusion(f32[8192,128]{1,0:T(8,128)} %all-gather.8.cloned.1.call-done, f32[2,1024,128]{2,1,0:T(8,128)S(1)} %copy-done), kind=kOutput, calls=%fused_computation.21 | convolution fusion | flops 12884901888 | bytes 38273024 | tf_op jit(solution)/shard_map/dot_general | solution.py:15
  841.3 44.7 %fusion = f32[8192,1024]{0,1:T(8,128)} fusion(f32[8192,1024]{0,1:T(8,128)} %fusion.7, f32[8192,1024]{0,1:T(8,128)} %fusion.1, f32[1024,128]{1,0:T(8,128)} %all-reduce.14.cloned.1.call-done, f32[2,8192,128]{2,1,0:T(8,128)} %all-gather.4.cloned.1.call-done), kind=kOutput, calls=%fused_computation.1 | convolution fusion | flops 12901679104 | bytes 105381888 | tf_op jit(solution)/shard_map/dot_general | solution.py:15
  886.0 33.4 %copy.9 = f32[8192,1024]{1,0:T(8,128)} copy(f32[8192,1024]{0,1:T(8,128)} %fusion) | data formatting | bytes 67108864 | tf_op jit(solution)/shard_map/sub | solution.py:51
  (8 shorter events, 0.0 us)
Async XLA Ops:
  6.5 235.2 %copy-start.1 = (f32[2,512,128]{2,1,0:T(8,128)S(1)}, f32[2,512,128]{2,1,0:T(8,128)}, u32[]{:S(2)}) copy-start(f32[2,512,128]{2,1,0:T(8,128)} %param.4) | copy-start | bytes 1572868
  6.5 233.6 %copy-start.2 = (f32[2,128,128]{2,1,0:T(8,128)S(1)}, f32[2,128,128]{2,1,0:T(8,128)}, u32[]{:S(2)}) copy-start(f32[2,128,128]{2,1,0:T(8,128)} %param.5) | copy-start | bytes 393220
  6.5 80.7 %all-gather.4.cloned.1.call-start = ((), (), s32[]{:S(2)}) async-start(), calls=%async_computation.2 | async-start | bytes 8912896 | tf_op jit(solution)/shard_map/all_gather | solution.py:27
  7.3 120.7 %all-reduce.6.cloned.1.call-start = ((), (), s32[]{:S(2)}) async-start(), calls=%async_computation.3 | async-start | bytes 2097152 | tf_op jit(solution)/shard_map/psum | solution.py:11
  89.5 150.7 %reduce-scatter.3.cloned.1.call-start = ((), (), s32[]{:S(2)}) async-start(), calls=%async_computation.4 | async-start | bytes 4456448 | tf_op jit(solution)/shard_map/reduce_scatter | solution.py:40
  167.6 194.6 %all-reduce.8.cloned.1.call-start = ((), (), s32[]{:S(2)}) async-start(), calls=%async_computation.5 | async-start | bytes 131072 | tf_op jit(solution)/shard_map/psum | solution.py:47
  243.0 173.0 %all-gather.6.cloned.1.call-start = ((), (), s32[]{:S(2)}) async-start(), calls=%async_computation.6 | async-start | bytes 4456448 | tf_op jit(solution)/shard_map/all_gather | solution.py:49
  364.5 53.7 %copy-start = (f32[2,1024,128]{2,1,0:T(8,128)S(1)}, f32[2,1024,128]{2,1,0:T(8,128)}, u32[]{:S(2)}) copy-start(f32[2,1024,128]{2,1,0:T(8,128)} %all-reduce.6.cloned.1.call-done) | copy-start | bytes 3145732
  364.5 85.2 %all-reduce.10.cloned.1.call-start = ((), (), s32[]{:S(2)}) async-start(), calls=%async_computation.7 | async-start | bytes 1048576 | tf_op jit(solution)/shard_map/psum | solution.py:11
  417.9 214.3 %reduce-scatter.5.cloned.1.call-start = ((), (), s32[]{:S(2)}) async-start(), calls=%async_computation.8 | async-start | bytes 4456448 | tf_op jit(solution)/shard_map/reduce_scatter | solution.py:40
  561.1 193.2 %all-reduce.12.cloned.1.call-start = ((), (), s32[]{:S(2)}) async-start(), calls=%async_computation.9 | async-start | bytes 131072 | tf_op jit(solution)/shard_map/psum | solution.py:47
  634.8 173.3 %all-gather.8.cloned.1.call-start = ((), (), s32[]{:S(2)}) async-start(), calls=%async_computation.10 | async-start | bytes 4456448 | tf_op jit(solution)/shard_map/all_gather | solution.py:49
  756.6 84.7 %all-reduce.14.cloned.1.call-start = ((), (), s32[]{:S(2)}) async-start(), calls=%async_computation.11 | async-start | bytes 1048576 | tf_op jit(solution)/shard_map/psum | solution.py:11
Sparse Core Ops, SparseCore 0:
  9.5 77.6 all-gather.3
  89.6 38.2 all-reduce.5
  167.7 72.3 reduce-scatter.2
  245.6 116.5 all-reduce.7
  364.6 51.3 all-gather.5
  418.2 27.0 all-reduce.9
  561.2 70.9 reduce-scatter.4
  637.8 116.4 all-reduce.11
  756.7 51.3 all-gather.7
  810.3 27.0 all-reduce.13
where the time goes:
time: 935 us; the launch traced here: 927 us
  waiting for transfers between devices  573 us (61%)
  matrix products  268 us (29%)
  local copies, waits for them, and re-layouts  64.6 us (7%)
  between operations  14.1 us (2%)
    dot_general x14, matrix products, mat_product(): jnp.dot(left, right, precision=highest, preferred_element_type=jnp.float32)  268 us
    psum x2, waiting for transfers between devices, body(): gram_matrix = lax.psum(mat_product(own_rows.T, ymatrix), ('row', 'col'))  239 us
    reduce_scatter x2, waiting for transfers between devices, body(): lax.psum_scatter(partial_rows(jnp.int32(0), own_count * lax.axis_size('co...  144 us
    all_gather x1, waiting for transfers between devices, body(): v_rows = lax.all_gather(vectors, 'col', axis=1, tiled=True)  79.9 us
    all_gather x2, waiting for transfers between devices, body(): w_i = lax.all_gather(w_own, 'col', axis=0, tiled=True)  71.8 us
    psum x3, waiting for transfers between devices, spread(): return lax.psum(block, axis)  38.4 us
    sub x1, local copies, waits for them, and re-layouts, body(): current - mat_product(vector_i, w_j.T) - mat_product(w_i, vector_j.T)  33.4 us
    unnamed x7, local copies, waits for them, and re-layouts  31.2 us
  transfers between devices with their start and end apart: 10, of which 8 were waited for; matrix products, arithmetic and copies ran while one was open for 10% of the time, Pallas kernels for 0%

commit v1 on v0

v1 whole, which is shorter than its diff:
```python
import functools

import jax
import jax.numpy as jnp
from jax import lax
from jax.experimental import pallas as pl
from jax.experimental.pallas import tpu as pltpu
from jax.sharding import PartitionSpec as P

highest = lax.Precision.HIGHEST
f32 = jnp.float32
bf16 = jnp.bfloat16
VMEM_LIMIT = 48 * 1024 * 1024


def split(value):
    high = value.astype(bf16)
    low = (value - high.astype(f32)).astype(bf16)
    return high, low


def dot(left, right):
    return jnp.dot(left, right, preferred_element_type=f32)


def exact(left, right):
    return jnp.dot(left, right, precision=highest, preferred_element_type=f32)


def exact_nt(left, right):
    return lax.dot_general(left, right, (((1,), (1,)), ((), ())), precision=highest, preferred_element_type=f32)


def row_block(rows):
    return min(rows, 512)


def product_kernel(a_ref, v_ref, out_ref):
    @pl.when(pl.program_id(0) == 0)
    def _():
        out_ref[...] = jnp.zeros_like(out_ref)

    v = jnp.concatenate([v_ref[p] for p in range(v_ref.shape[0])], axis=1)
    v_hi, v_lo = split(v.T)
    a_hi, a_lo = split(a_ref[...])
    wide = v_hi.shape[0]
    both = dot(jnp.concatenate([v_hi, v_lo], axis=0), a_hi)
    out_ref[...] += both[:wide] + (both[wide:] + dot(v_hi, a_lo))


def product(a, v):
    rows, cols = a.shape
    panels, _, b = v.shape
    block = row_block(rows)
    return pl.pallas_call(
        product_kernel,
        grid=(rows // block,),
        in_specs=[
            pl.BlockSpec((block, cols), lambda i: (i, 0)),
            pl.BlockSpec((panels, block, b), lambda i: (0, i, 0)),
        ],
        out_specs=pl.BlockSpec((panels * b, cols), lambda i: (0, 0)),
        out_shape=jax.ShapeDtypeStruct((panels * b, cols), f32),
        compiler_params=pltpu.CompilerParams(vmem_limit_bytes=VMEM_LIMIT),
        name="product",
    )(a, v)


def sum_rows(mine, other):
    wide, cols = mine.shape

    def kernel(mine_ref, other_ref, sum_ref, z_ref):
        total = mine_ref[...] + other_ref[...]
        sum_ref[...] = total
        z_ref[...] = total.T

    return pl.pallas_call(
        kernel,
        out_shape=(jax.ShapeDtypeStruct((wide, cols), f32), jax.ShapeDtypeStruct((cols, wide), f32)),
        compiler_params=pltpu.CompilerParams(vmem_limit_bytes=VMEM_LIMIT),
        name="sum_rows",
    )(mine, other)


def gram_kernel(v_ref, z_ref, out_ref, cross_ref):
    @pl.when(pl.program_id(0) == 0)
    def _():
        out_ref[...] = jnp.zeros_like(out_ref)
        cross_ref[...] = jnp.zeros_like(cross_ref)

    v = jnp.concatenate([v_ref[p] for p in range(v_ref.shape[0])], axis=1)
    vt_hi, vt_lo = split(v.T)
    v_hi, v_lo = split(v)
    z_hi, z_lo = split(z_ref[...])
    b = v_ref.shape[2]
    out_ref[...] += dot(vt_hi, z_hi) + (dot(vt_lo, z_hi) + dot(vt_hi, z_lo))
    cross_ref[...] += dot(vt_hi[:b], v_hi[:, b:]) + (dot(vt_lo[:b], v_hi[:, b:]) + dot(vt_hi[:b], v_lo[:, b:]))


def gram(v, z):
    panels, rows, b = v.shape
    wide = panels * b
    block = row_block(rows)
    return pl.pallas_call(
        gram_kernel,
        grid=(rows // block,),
        in_specs=[
            pl.BlockSpec((panels, block, b), lambda i: (0, i, 0)),
            pl.BlockSpec((block, wide), lambda i: (i, 0)),
        ],
        out_specs=[
            pl.BlockSpec((wide, wide), lambda i: (0, 0)),
            pl.BlockSpec((b, b), lambda i: (0, 0)),
        ],
        out_shape=(jax.ShapeDtypeStruct((wide, wide), f32), jax.ShapeDtypeStruct((b, b), f32)),
        compiler_params=pltpu.CompilerParams(vmem_limit_bytes=VMEM_LIMIT),
        name="gram",
    )(v, z)


def factor_kernel(t_ref, m_ref, n_ref, zt_ref, vc_ref, hi_ref, lo_ref):
    b = t_ref.shape[1]
    upper = lax.broadcasted_iota(jnp.int32, (b, b), 0) <= lax.broadcasted_iota(jnp.int32, (b, b), 1)
    t1 = jnp.where(upper, t_ref[0], 0.0)
    t2 = jnp.where(upper, t_ref[1], 0.0)
    n = n_ref[...]
    m11, m12, m22 = m_ref[:b, :b], m_ref[:b, b:], m_ref[b:, b:]
    k1 = exact(t1.T, exact(m11, t1))
    e = exact(t1.T, m12) - 0.5 * exact(k1.T, n)
    nte = exact(n.T, e)
    k2 = exact(t2.T, exact(m22 - nte - nte.T, t2))
    s12 = -exact(t1, exact(n, t2))
    r11 = -0.5 * k1
    r12 = exact(0.5 * exact(k1, n) - e, t2)
    r22 = -0.5 * k2
    s = jnp.concatenate([jnp.concatenate([t1, s12], 1), jnp.concatenate([jnp.zeros_like(t1), t2], 1)], 0)
    r = jnp.concatenate([jnp.concatenate([r11 + r11.T, r12], 1), jnp.concatenate([r12.T, r22 + r22.T], 1)], 0)
    vct = jnp.concatenate([vc_ref[0], vc_ref[1]], axis=1).T
    pt = exact(s.T, zt_ref[...]) + exact(r, vct)
    qt = exact(s, vct)
    wide = 2 * b
    hi_ref[:wide], lo_ref[:wide] = split(pt)
    hi_ref[wide:], lo_ref[wide:] = split(qt)


def factors(tfactor, m, n, zt, vc):
    wide, cols = zt.shape
    out = jax.ShapeDtypeStruct((2 * wide, cols), bf16)
    return pl.pallas_call(
        factor_kernel,
        out_shape=(out, out),
        compiler_params=pltpu.CompilerParams(vmem_limit_bytes=VMEM_LIMIT),
        name="factors",
    )(tfactor, m, n, zt, vc)


def update_kernel(a_ref, v_ref, z_ref, hi_ref, lo_ref, out_ref):
    left = jnp.concatenate([v_ref[p] for p in range(v_ref.shape[0])] + [z_ref[...]], axis=1)
    l_hi, l_lo = split(left)
    hi = hi_ref[...]
    out_ref[...] = a_ref[...] - (dot(l_hi, hi) + (dot(l_lo, hi) + dot(l_hi, lo_ref[...])))


def update(a, v, z, hi, lo):
    rows, cols = a.shape
    panels, _, b = v.shape
    block = row_block(rows)
    wide = panels * b
    return pl.pallas_call(
        update_kernel,
        grid=(rows // block,),
        in_specs=[
            pl.BlockSpec((block, cols), lambda i: (i, 0)),
            pl.BlockSpec((panels, block, b), lambda i: (0, i, 0)),
            pl.BlockSpec((block, wide), lambda i: (i, 0)),
            pl.BlockSpec((2 * wide, cols), lambda i: (0, 0)),
            pl.BlockSpec((2 * wide, cols), lambda i: (0, 0)),
        ],
        out_specs=pl.BlockSpec((block, cols), lambda i: (i, 0)),
        out_shape=jax.ShapeDtypeStruct((rows, cols), f32),
        compiler_params=pltpu.CompilerParams(vmem_limit_bytes=VMEM_LIMIT),
        name="update",
    )(a, v, z, hi, lo)


def row_sum(value):
    total = lax.axis_size("row")
    if total == 2:
        return lax.ppermute(value, "row", [(0, 1), (1, 0)])
    return lax.psum(value, "row") - value


def body(matrix, vectors, tfactor):
    rows_here, cols_here = matrix.shape
    own = vectors.shape[1]
    row_total, col_total = lax.axis_size("row"), lax.axis_size("col")
    row, col = lax.axis_index("row"), lax.axis_index("col")
    owner = col * row_total // col_total
    offset = col * cols_here - owner * rows_here

    v_rows = lax.all_gather(vectors, "col", axis=1, tiled=True)
    mine = lax.dynamic_slice_in_dim(v_rows, offset, cols_here, 1)
    v_cols = mine
    for shift in range(1, row_total):
        other = lax.ppermute(mine, "row", [(i, (i + shift) % row_total) for i in range(row_total)])
        v_cols = jnp.where((row - owner) % row_total == shift, other, v_cols)

    part = product(matrix, v_rows)
    zt, z = sum_rows(part, row_sum(part))

    per_row = col_total // row_total
    z_own = None
    for piece in range(row_total):
        pairs = []
        for r in range(row_total):
            for c in range(per_row):
                pairs.append((r * col_total + r * per_row + c, r * col_total + c * row_total + piece))
        sent = lax.ppermute(z[piece * own : (piece + 1) * own], ("row", "col"), pairs)
        z_own = sent if z_own is None else z_own + sent
    z_rows = lax.all_gather(z_own, "col", axis=0, tiled=True)

    m, n = gram(v_rows, z_rows)
    small = jnp.concatenate([m, jnp.concatenate([n, jnp.zeros_like(n)], 1)], 0)
    small = small + row_sum(small)
    b = n.shape[0]
    hi, lo = factors(tfactor, small[: 2 * b], small[2 * b :, :b], zt, v_cols)
    return update(matrix, v_rows, z_rows, hi, lo)


def solution(mesh):
    return jax.shard_map(
        body,
        mesh=mesh,
        in_specs=(P("row", "col"), P(None, ("row", "col"), None), P()),
        out_specs=P("row", "col"),
        check_vma=False,
    )
```

time: 935 us -> 315 us (0.34)
  waiting for transfers between devices: 573 us -> 184 us
  matrix products: 268 us -> 0 us
  Pallas kernels: 0 us -> 82.1 us
  local copies, waits for them, and re-layouts: 64.6 us -> 1.41 us
  starting transfers between devices: 0.63 us -> 31.1 us
    psum x5 -> x0, waiting for transfers between devices: 277 us -> none  [the longest x2 239 us: body(): gram_matrix = lax.psum(mat_product(own_rows.T, ymatrix), ('row', 'col'))]
    dot_general x14 -> x0, matrix products: 268 us -> none  [mat_product(): jnp.dot(left, right, precision=highest, preferred_element_type=jnp.float32)]
    reduce_scatter x2 -> x0, waiting for transfers between devices: 144 us -> none  [body(): lax.psum_scatter(partial_rows(jnp.int32(0), own_count * lax.axis_size('co...]
    pallas_call x0 -> x5, Pallas kernels: none -> 82.1 us  [the longest x1 38.5 us: update(): pl.pallas_call(update_kernel, grid=(rows // block,), in_specs=[pl.BlockSp...]
    sub x1 -> x0, local copies, waits for them, and re-layouts: 33.4 us -> none  [body(): current - mat_product(vector_i, w_j.T) - mat_product(w_i, vector_j.T)]
    ppermute x0 -> x5, waiting for transfers between devices: none -> 33.1 us  [the longest x2 32.3 us: row_sum(): return lax.ppermute(value, 'row', [(0, 1), (1, 0)])]
    unnamed x7 -> x2, local copies, waits for them, and re-layouts: 31.2 us -> 0.01 us
    ppermute x0 -> x5, starting transfers between devices: none -> 31.1 us  [the longest x1 25.9 us: body(): lax.ppermute(mine, 'row', [(i, (i + shift) % row_total) for i in range(ro...]
  transfers between devices with their start and end apart: 10 -> 7, of which waited for: 8 -> 5; matrix products, arithmetic and copies ran while one was open for 10% -> 1% of each run, Pallas kernels for 0% -> 5%
where the time goes in v1:
time: 315 us; the launch traced here: 314 us
  waiting for transfers between devices  184 us (58%)
  Pallas kernels  82.1 us (26%)
  starting transfers between devices  31.1 us (10%)
  between operations  13.5 us (4%)
    all_gather x1, waiting for transfers between devices, body(): v_rows = lax.all_gather(vectors, 'col', axis=1, tiled=True)  79.9 us
    all_gather x1, waiting for transfers between devices, body(): z_rows = lax.all_gather(z_own, 'col', axis=0, tiled=True)  69.9 us
    pallas_call x1, Pallas kernels, update(): pl.pallas_call(update_kernel, grid=(rows // block,), in_specs=[pl.BlockSp...  38.5 us
    ppermute x2, waiting for transfers between devices, row_sum(): return lax.ppermute(value, 'row', [(0, 1), (1, 0)])  32.3 us
    ppermute x1, starting transfers between devices, body(): lax.ppermute(mine, 'row', [(i, (i + shift) % row_total) for i in range(ro...  25.9 us
    pallas_call x1, Pallas kernels, product(): pl.pallas_call(product_kernel, grid=(rows // block,), in_specs=[pl.BlockS...  23.7 us
    pallas_call x1, Pallas kernels, gram(): pl.pallas_call(gram_kernel, grid=(rows // block,), in_specs=[pl.BlockSpec...  15.1 us
  transfers between devices with their start and end apart: 7, of which 5 were waited for; matrix products, arithmetic and copies ran while one was open for 1% of the time, Pallas kernels for 5%

profile of v1, /device:TPU:0, one launch (start us, length us, event | category | flops | bytes accessed | tf_op | source)
XLA Modules:
  0.0 314.0 jit_solution(11282424623203816892)
XLA Ops:
  6.5 0.0 all-gather.3.cloned.1.call-start
  6.5 0.7 all-gather.3.cloned.1.call-update
  7.3 0.0 all-gather.5.cloned.1.call-start
  7.3 79.9 %all-gather.3.cloned.1.call-done.v_ref = f32[2,8192,128]{2,1,0:T(8,128)} async-done(((f32[2,512,128]{2,1,0:T(8,128)}), f32[2,8192,128]{2,1,0:T(8,128)}) %all-gather.3.cloned.1.call-update) | async-done | bytes 8388624 | tf_op jit(solution)/shard_map/all_gather | solution.py:201
  87.2 23.7 %product.1.mine_ref = f32[256,1024]{1,0:T(8,128)S(1)} custom-call(f32[8192,1024]{1,0:T(8,128)} %a_ref.3, f32[2,8192,128]{2,1,0:T(8,128)} %all-gather.3.cloned.1.call-done.v_ref), custom_call_target="tpu_custom_call" | custom-call | tf_op jit(solution)/shard_map/product/pallas_call | solution.py:55
  110.9 1.5 collective-permute-start
  112.5 23.9 %collective-permute-done.other_ref = f32[256,1024]{1,0:T(8,128)S(1)} collective-permute-done((f32[256,1024]{1,0:T(8,128)S(1)}, f32[256,1024]{1,0:T(8,128)S(1)}, u32[]{:S(2)}, u32[]{:S(2)}) %collective-permute-start) | collective-permute-done | bytes 1048608 | tf_op jit(solution)/shard_map/ppermute | solution.py:189
  136.3 0.3 sum_rows.1
  136.7 0.1 fusion.1
  136.7 1.4 collective-permute-start.2
  138.1 0.7 collective-permute-start.1
  138.8 0.8 collective-permute-done.2
  139.6 0.0 collective-permute-done.1
  139.6 0.9 add.16
  140.5 0.0 all-gather.5.cloned.1.call-update
  140.5 1.3 constant_dynamic-slice_fusion
  141.8 0.0 copy-start
  141.9 25.9 %collective-permute-start.4 = (f32[2,1024,128]{2,1,0:T(8,128)S(1)}, f32[2,1024,128]{2,1,0:T(8,128)}, u32[]{:S(2)}, u32[]{:S(2)}) collective-permute-start(f32[2,1024,128]{2,1,0:T(8,128)S(1)} %constant_dynamic-slice_fusion), channel_id=1, source_target_pairs={{0,16},{16,0},{1,17},{17,1},{2,18},{18,2},{3,19},{19,3},{4,20},{20... | collective-permute-start | bytes 3145736 | tf_op jit(solution)/shard_map/ppermute | solution.py:205
  167.8 69.9 %all-gather.5.cloned.1.call-done.z_ref = f32[8192,256]{1,0:T(8,128)} async-done(((f32[512,256]{1,0:T(8,128)}), f32[8192,256]{1,0:T(8,128)}) %all-gather.5.cloned.1.call-update) | async-done | bytes 8388624 | tf_op jit(solution)/shard_map/all_gather | solution.py:220
  237.7 15.1 %gram.1 = (f32[256,256]{1,0:T(8,128)S(1)}, f32[128,128]{1,0:T(8,128)S(1)}) custom-call(f32[2,8192,128]{2,1,0:T(8,128)} %all-gather.3.cloned.1.call-done.v_ref, f32[8192,256]{1,0:T(8,128)} %all-gather.5.cloned.1.call-done.z_ref), custom_call_target="tpu_custom_call" | custom-call | tf_op jit(solution)/shard_map/gram/pallas_call | solution.py:104
  252.8 1.5 collective-permute-start.3
  254.3 0.0 collective-permute-done.4
  254.3 1.3 broadcast_select_fusion.vc_ref
  255.7 8.5 %collective-permute-done.3 = f32[384,256]{1,0:T(8,128)S(1)} collective-permute-done((f32[384,256]{1,0:T(8,128)S(1)}, f32[384,256]{1,0:T(8,128)S(1)}, u32[]{:S(2)}, u32[]{:S(2)}) %collective-permute-start.3) | collective-permute-done | bytes 393248 | tf_op jit(solution)/shard_map/ppermute | solution.py:189
  264.2 0.0 copy-done
  264.3 4.4 %factors.1 = (bf16[512,1024]{1,0:T(8,128)(2,1)S(1)}, bf16[512,1024]{1,0:T(8,128)(2,1)S(1)}) custom-call(f32[2,128,128]{2,1,0:T(8,128)S(1)} %copy-done, f32[256,256]{1,0:T(8,128)S(1)} %slice.16.m_ref, f32[128,128]{1,0:T(8,128)S(1)} %slice.17.n_ref, f32[256,1024]{1,0:T(8,128)S(1)} %get-tuple-element.14.zt_ref, f32[2,1024,128]{2,1,0:T(8,128)S(1)} %broadcast_select_fusion.vc_ref), custom_call_target="tpu_custom_call" | custom-call | tf_op jit(solution)/shard_map/factors/pallas_call | solution.py:149
  268.7 38.5 %update.1 = f32[8192,1024]{1,0:T(8,128)} custom-call(f32[8192,1024]{1,0:T(8,128)} %a_ref.3, f32[2,8192,128]{2,1,0:T(8,128)} %all-gather.3.cloned.1.call-done.v_ref, f32[8192,256]{1,0:T(8,128)} %all-gather.5.cloned.1.call-done.z_ref, bf16[512,1024]{1,0:T(8,128)(2,1)S(1)} %get-tuple-element.15.hi_ref, bf16[512,1024]{1,0:T(8,128)(2,1)S(1)} %get-tuple-element.16.lo_ref), custom_call_target="tpu_custom_call" | custom-call | tf_op jit(solution)/shard_map/update/pallas_call | solution.py:169
  (4 shorter events, 0.1 us)
Async XLA Ops:
  6.5 80.7 %all-gather.3.cloned.1.call-start = ((), (), s32[]{:S(2)}) async-start(), calls=%async_computation | async-start | bytes 8912896 | tf_op jit(solution)/shard_map/all_gather | solution.py:201
  7.3 230.4 %all-gather.5.cloned.1.call-start = ((), (), s32[]{:S(2)}) async-start(), calls=%async_computation.1 | async-start | bytes 8912896 | tf_op jit(solution)/shard_map/all_gather | solution.py:220
  110.9 25.4 %collective-permute-start = (f32[256,1024]{1,0:T(8,128)S(1)}, f32[256,1024]{1,0:T(8,128)S(1)}, u32[]{:S(2)}, u32[]{:S(2)}) collective-permute-start(f32[256,1024]{1,0:T(8,128)S(1)} %product.1.mine_ref), channel_id=1, source_target_pairs={{0,16},{16,0},{1,17},{17,1},{2,18},{18,2},{3,19},{19,3},{4,20},{20... | collective-permute-start | bytes 3145736 | tf_op jit(solution)/shard_map/ppermute | solution.py:189
  136.7 2.9 collective-permute-start.2
  138.1 1.5 collective-permute-start.1
  141.8 122.4 %copy-start = (f32[2,128,128]{2,1,0:T(8,128)S(1)}, f32[2,128,128]{2,1,0:T(8,128)}, u32[]{:S(2)}) copy-start(f32[2,128,128]{2,1,0:T(8,128)} %t_ref.1) | copy-start | bytes 393220
  141.9 112.5 %collective-permute-start.4 = (f32[2,1024,128]{2,1,0:T(8,128)S(1)}, f32[2,1024,128]{2,1,0:T(8,128)}, u32[]{:S(2)}, u32[]{:S(2)}) collective-permute-start(f32[2,1024,128]{2,1,0:T(8,128)S(1)} %constant_dynamic-slice_fusion), channel_id=1, source_target_pairs={{0,16},{16,0},{1,17},{17,1},{2,18},{18,2},{3,19},{19,3},{4,20},{20... | collective-permute-start | bytes 3145736 | tf_op jit(solution)/shard_map/ppermute | solution.py:205
  252.8 11.3 %collective-permute-start.3 = (f32[384,256]{1,0:T(8,128)S(1)}, f32[384,256]{1,0:T(8,128)S(1)}, u32[]{:S(2)}, u32[]{:S(2)}) collective-permute-start(f32[384,256]{1,0:T(8,128)S(1)} %select_maximum_fusion), channel_id=1, source_target_pairs={{0,16},{16,0},{1,17},{17,1},{2,18},{18,2},{3,19},{19,3},{4,20},{20... | collective-permute-start | bytes 1179656 | tf_op jit(solution)/shard_map/ppermute | solution.py:189
Sparse Core Ops, SparseCore 0:
  9.5 77.6 all-gather.2
  140.6 97.0 all-gather.4

commit v2 on v1

--- a/solution.py
+++ b/solution.py
@@ -190,7 +190,7 @@
     return lax.psum(value, "row") - value
 
 
-def body(matrix, vectors, tfactor):
+def general_body(matrix, vectors, tfactor):
     rows_here, cols_here = matrix.shape
     own = vectors.shape[1]
     row_total, col_total = lax.axis_size("row"), lax.axis_size("col")
@@ -227,9 +227,277 @@
     return update(matrix, v_rows, z_rows, hi, lo)
 
 
+def ring_chip(position, chips):
+    position %= chips
+    return 2 * position if position < chips // 2 else 2 * (chips - 1 - position) + 1
+
+
+def ring_chips_here(chips, steps):
+    chip = lax.axis_index("col") // 2
+    place = jnp.where(chip % 2 == 0, chip // 2, chips - 1 - chip // 2)
+
+    def at(position):
+        position = position % chips
+        return jnp.where(position < chips // 2, 2 * position, 2 * (chips - 1 - position) + 1)
+
+    core = lax.axis_index("col") % 2
+    signs = 2 * core - 1
+    return [at(place + signs * step) for step in steps], [at(place - signs * step) for step in steps]
+
+
+def ring_gather(streams):
+    chips = lax.axis_size("col") // 2
+    core = lax.axis_index("col") % 2
+    swap = [(c, c ^ 1) for c in range(2 * chips)]
+    around = []
+    for i in range(chips):
+        around.append((2 * ring_chip(i, chips), 2 * ring_chip(i + 1, chips)))
+        around.append((2 * ring_chip(i, chips) + 1, 2 * ring_chip(i - 1, chips) + 1))
+
+    def joined(mine):
+        other = lax.ppermute(mine, "col", swap)
+        first, second = jnp.where(core == 0, mine, other), jnp.where(core == 0, other, mine)
+        return jnp.concatenate([first, second], axis=0)
+
+    held = [joined(mine) for mine in streams]
+    result = [[block] for block in held]
+    for _ in range(1, chips // 2):
+        held = [lax.ppermute(block, "col", around) for block in held]
+        for blocks, block in zip(result, held):
+            blocks += [block, lax.ppermute(block, "col", swap)]
+    for blocks, block in zip(result, held):
+        rows = block.shape[0] // 2
+        part = lax.dynamic_slice_in_dim(block, core * rows, rows, 0)
+        blocks.append(joined(lax.ppermute(part, "col", around)))
+    return result
+
+
+def ring_order(chips):
+    came, other = ring_chips_here(chips, range(chips // 2 + 1))
+    order = [came[0]]
+    for step in range(1, chips // 2):
+        order += [came[step], other[step]]
+    return order + [came[chips // 2]]
+
+
+def part_kernel(count, first, index_ref, a_ref, *refs):
+    values, refs = refs[: 2 * count], refs[2 * count :]
+    if first:
+        out_ref, v_ref = refs
+    else:
+        total_ref, _, out_ref, v_ref = refs
+    step = pl.program_id(0)
+
+    @pl.when(step == 0)
+    def _():
+        out_ref[...] = jnp.zeros_like(out_ref) if first else total_ref[...]
+
+    for j in range(count):
+
+        @pl.when(step == j)
+        def _(j=j):
+            v_ref[...] = jnp.concatenate([values[2 * j][...], values[2 * j + 1][...]], axis=1)
+
+    v_hi, v_lo = split(v_ref[...].T)
+    a_hi, a_lo = split(a_ref[...])
+    wide = v_hi.shape[0]
+    both = dot(jnp.concatenate([v_hi, v_lo], axis=0), a_hi)
+    out_ref[...] += both[:wide] + (both[wide:] + dot(v_hi, a_lo))
+
+
+def part_product(a, blocks, index, state):
+    rows, cols = a.shape
+    block, b = blocks[0][0].shape
+    count = len(blocks)
+    first = state is None
+    wide = 2 * b
+    whole = pl.BlockSpec((block, b), lambda i, index: (0, 0))
+    total = pl.BlockSpec((wide, cols), lambda i, index: (0, 0))
+    in_specs = [pl.BlockSpec((block, cols), lambda i, index: (index[i], 0))] + [whole] * (2 * count)
+    operands = [value for pair in blocks for value in pair]
+    aliases = {}
+    if not first:
+        in_specs += [total, pl.BlockSpec(memory_space=pl.ANY)]
+        operands += list(state)
+        aliases = {2 + 2 * count: 0, 3 + 2 * count: 1}
+    return pl.pallas_call(
+        functools.partial(part_kernel, count, first),
+        grid_spec=pltpu.PrefetchScalarGridSpec(
+            num_scalar_prefetch=1,
+            grid=(count,),
+            in_specs=in_specs,
+            out_specs=[total, pl.BlockSpec((block, wide), lambda i, index: (index[i], 0))],
+        ),
+        out_shape=(jax.ShapeDtypeStruct((wide, cols), f32), jax.ShapeDtypeStruct((rows, wide), f32)),
+        input_output_aliases=aliases,
+        compiler_params=pltpu.CompilerParams(vmem_limit_bytes=VMEM_LIMIT),
+        name="part_product",
+    )(index, a, *operands)
+
+
+def own_gram_kernel(index_ref, v_ref, z1_ref, z2_ref, out_ref):
+    b = z1_ref.shape[1]
+    v = v_ref[...]
+    vt = v.T
+    z = jnp.concatenate([z1_ref[...], z2_ref[...]], axis=1)
+    out_ref[:b] = exact(vt[:b], z)
+    out_ref[b:, :b] = exact(vt[:b], v[:, b:])
+    out_ref[b:, b:] = exact(vt[b:], z[:, b:])
+
+
+def own_gram(index, v, z1, z2):
+    rows, b = z1.shape
+    return pl.pallas_call(
+        own_gram_kernel,
+        grid_spec=pltpu.PrefetchScalarGridSpec(
+            num_scalar_prefetch=1,
+            grid=(1,),
+            in_specs=[
+                pl.BlockSpec((rows, 2 * b), lambda i, index: (index[0], 0)),
+                pl.BlockSpec((rows, b), lambda i, index: (0, 0)),
+                pl.BlockSpec((rows, b), lambda i, index: (0, 0)),
+            ],
+            out_specs=pl.BlockSpec((2 * b, 2 * b), lambda i, index: (0, 0)),
+        ),
+        out_shape=jax.ShapeDtypeStruct((2 * b, 2 * b), f32),
+        compiler_params=pltpu.CompilerParams(vmem_limit_bytes=VMEM_LIMIT),
+        name="own_gram",
+    )(index, v, z1, z2)
+
+
+def part_update_kernel(count, first, index_ref, a_ref, v_ref, hi_ref, lo_ref, *refs):
+    values, out_ref = refs[: 2 * count], refs[-1]
+    step = pl.program_id(0)
+    rows = a_ref.shape[0]
+    hi, lo = hi_ref[...], lo_ref[...]
+    for j in range(2 * count):
+
+        @pl.when(step == j)
+        def _(j=j):
+            here = pl.ds((j % 2) * rows, rows)
+            left = jnp.concatenate([v_ref[...], values[j // 2 * 2][here, :], values[j // 2 * 2 + 1][here, :]], axis=1)
+            l_hi, l_lo = split(left)
+            out_ref[...] = a_ref[...] - (dot(l_hi, hi) + (dot(l_lo, hi) + dot(l_hi, lo)))
+
+
+def part_update(a, v, hi, lo, blocks, index, state):
+    rows, cols = a.shape
+    wide = v.shape[1]
+    count = len(blocks)
+    span, b = blocks[0][0].shape
+    block = span // 2
+    first = state is None
+    placed = lambda i, index: (index[i], 0)
+    fixed = lambda i, index: (0, 0)
+    in_specs = [
+        pl.BlockSpec((block, cols), placed),
+        pl.BlockSpec((block, wide), placed),
+        pl.BlockSpec((2 * wide, cols), fixed),
+        pl.BlockSpec((2 * wide, cols), fixed),
+    ] + [pl.BlockSpec((span, b), fixed)] * (2 * count)
+    operands = [a, v, hi, lo] + [value for pair in blocks for value in pair]
+    aliases = {}
+    if not first:
+        in_specs.append(pl.BlockSpec(memory_space=pl.ANY))
+        operands.append(state)
+        aliases = {len(operands): 0}
+    return pl.pallas_call(
+        functools.partial(part_update_kernel, count, first),
+        grid_spec=pltpu.PrefetchScalarGridSpec(
+            num_scalar_prefetch=1,
+            grid=(2 * count,),
+            in_specs=in_specs,
+            out_specs=pl.BlockSpec((block, cols), placed),
+        ),
+        out_shape=jax.ShapeDtypeStruct((rows, cols), f32),
+        input_output_aliases=aliases,
+        compiler_params=pltpu.CompilerParams(vmem_limit_bytes=VMEM_LIMIT),
+        name="part_update",
+    )(index, *operands)
+
+
+def all_sum(value):
+    cols = lax.axis_size("col")
+    core = lax.axis_index("col") % 2
+    swap = [(c, c ^ 1) for c in range(cols)]
+    rows = value.shape[0] // 2
+    keep = lax.dynamic_slice_in_dim(value, core * rows, rows, 0)
+    give = lax.dynamic_slice_in_dim(value, (1 - core) * rows, rows, 0)
+    keep = keep + lax.ppermute(give, "col", swap)
+    keep = keep + lax.ppermute(keep, "row", [(0, 1), (1, 0)])
+    bit = 2
+    while bit < cols:
+        keep = keep + lax.ppermute(keep, "col", [(c, c ^ bit) for c in range(cols)])
+        bit *= 2
+    other = lax.ppermute(keep, "col", swap)
+    return jnp.concatenate([jnp.where(core == 0, keep, other), jnp.where(core == 0, other, keep)], axis=0)
+
+
+def body(matrix, vectors, tfactor):
+    rows_here, cols_here = matrix.shape
+    own, b = vectors.shape[1:]
+    cols = lax.axis_size("col")
+    row, col = lax.axis_index("row"), lax.axis_index("col")
+    chips = cols // 2
+    half = chips // 2
+    chip, core = col // 2, col % 2
+    both = ("row", "col")
+
+    order = ring_order(chips)
+    v_blocks = list(zip(*ring_gather([vectors[0], vectors[1]])))
+    state = None
+    for begin, end in ((0, 3), (3, chips - 1), (chips - 1, chips)):
+        state = part_product(matrix, v_blocks[begin:end], jnp.stack(order[begin:end]).astype(jnp.int32), state)
+    part, v_rows = state
+
+    keep = lax.dynamic_slice_in_dim(part, row * own, own, 1)
+    give = lax.dynamic_slice_in_dim(part, (1 - row) * own, own, 1)
+    across = [(0, 1), (1, 0)]
+    sums = [keep[p * b : (p + 1) * b] + lax.ppermute(give[p * b : (p + 1) * b], "row", across) for p in range(2)]
+    halves = [s.T for s in sums]
+
+    def at(r, j, k):
+        return r * cols + 2 * (j % chips) + k
+
+    foreign = [(r, j, k) for r in range(2) for j in range((1 - r) * half, (2 - r) * half) for k in range(2)]
+    direct = [(at(r, j, k), at(1 - r, j + half, k)) for r, j, k in foreign]
+    along = [(at(r, j, k), at(r, j + half, k)) for r, j, k in foreign]
+    over = [(at(r, j + half, k), at(1 - r, j + half, k)) for r, j, k in foreign]
+    got1 = lax.ppermute(halves[0], both, direct)
+    got2 = lax.ppermute(lax.ppermute(halves[1], both, along), both, over)
+    home = chip // half == row
+    z1 = jnp.where(home, halves[0], got1)
+    z2 = jnp.where(home, halves[1], got2)
+
+    def z_index(j, k):
+        return 2 * (2 * (j % half) + k) + j // half
+
+    small = all_sum(own_gram(z_index(chip, core).reshape(1).astype(jnp.int32), v_rows, z1, z2))
+
+    owner = col // chips
+    mine = lax.dynamic_slice_in_dim(v_rows, (col - owner * chips) * cols_here, cols_here, 0)
+    mine, _ = lax.optimization_barrier((mine, z1))
+    tile_pairs = [(r * cols + c, (1 - r) * cols + c) for r in range(2) for c in range(r * chips, (r + 1) * chips)]
+    v_cols = jnp.where(owner == row, mine, lax.ppermute(mine, both, tile_pairs))
+    sums = jnp.concatenate(sums, axis=0)
+    others = lax.ppermute(sums, "row", across)
+    zt = jnp.concatenate([jnp.where(row == 0, sums, others), jnp.where(row == 0, others, sums)], axis=1)
+
+    z_blocks = list(zip(*ring_gather([z1, z2])))
+    v_pair = jnp.stack([v_cols[:, :b], v_cols[:, b:]])
+    hi, lo = factors(tfactor, small, small[b:, :b], zt, v_pair)
+    out = None
+    for begin, end in ((0, chips - 3), (chips - 3, chips - 1), (chips - 1, chips)):
+        index = jnp.stack([z_index(j, k) for j in order[begin:end] for k in range(2)]).astype(jnp.int32)
+        out = part_update(matrix, v_rows, hi, lo, z_blocks[begin:end], index, out)
+    return out
+
+
 def solution(mesh):
+    rows, cols = mesh.shape["row"], mesh.shape["col"]
+    pairs = rows == 2 and cols >= 8 and cols & (cols - 1) == 0
     return jax.shard_map(
-        body,
+        body if pairs else general_body,
         mesh=mesh,
         in_specs=(P("row", "col"), P(None, ("row", "col"), None), P()),
         out_specs=P("row", "col"),

time: 315 us -> 236 us (0.75)
  waiting for transfers between devices: 184 us -> 78.6 us
  starting transfers between devices: 31.1 us -> 58.9 us
  between operations: 13.5 us -> 0.86 us
  local copies, waits for them, and re-layouts: 1.41 us -> 9.51 us
  other arithmetic: 2.26 us -> 7.55 us
    all_gather x2 -> x0, waiting for transfers between devices: 150 us -> none  [the longest x1 79.9 us: body(): v_rows = lax.all_gather(vectors, 'col', axis=1, tiled=True)]
    ppermute x5 -> x49, waiting for transfers between devices: 33.1 us -> 78.6 us  [the longest x12 32.7 us: ring_gather(): held = [lax.ppermute(block, 'col', around) for block in held]]
    ppermute x5 -> x49, starting transfers between devices: 31.1 us -> 58.9 us  [the longest x12 21.8 us: ring_gather(): held = [lax.ppermute(block, 'col', around) for block in held]]
    unnamed x2 -> x18, local copies, waits for them, and re-layouts: 0.01 us -> 4.02 us
    select_n x1 -> x12, other arithmetic: 1.33 us -> 4.83 us  [the longest x7 3.3 us: joined(): jnp.where(core == 0, mine, other)]
    pallas_call x4 -> x7, Pallas kernels: 77.7 us -> 75.3 us  [the longest x3 47.4 us: part_update(): pl.pallas_call(functools.partial(part_update_kernel, count, first), grid_...]
  transfers between devices with their start and end apart: 7 -> 49, of which waited for: 5 -> 19; matrix products, arithmetic and copies ran while one was open for 1% -> 4% of each run, Pallas kernels for 5% -> 24%
where the time goes in v2:
time: 236 us; the launch traced here: 235 us
  Pallas kernels  79.8 us (34%)
  waiting for transfers between devices  78.6 us (33%)
  starting transfers between devices  58.9 us (25%)
  local copies, waits for them, and re-layouts  9.51 us (4%)
  other arithmetic  7.55 us (3%)
    pallas_call x3, Pallas kernels, part_update(): pl.pallas_call(functools.partial(part_update_kernel, count, first), grid_...  47.4 us
    ppermute x12, waiting for transfers between devices, ring_gather(): held = [lax.ppermute(block, 'col', around) for block in held]  32.7 us
    pallas_call x3, Pallas kernels, part_product(): pl.pallas_call(functools.partial(part_kernel, count, first), grid_spec=pl...  26 us
    ppermute x12, starting transfers between devices, ring_gather(): held = [lax.ppermute(block, 'col', around) for block in held]  21.8 us
    ppermute x2, waiting for transfers between devices, body(): got2 = lax.ppermute(lax.ppermute(halves[1], both, along), both, over)  19.5 us
    ppermute x3, waiting for transfers between devices, all_sum(): keep = keep + lax.ppermute(keep, 'col', [(c, c ^ bit) for c in range(cols)])  14.8 us
    ppermute x2, starting transfers between devices, body(): lax.ppermute(give[p * b:(p + 1) * b], 'row', across)  7.11 us
    ppermute x2, waiting for transfers between devices, body(): lax.ppermute(give[p * b:(p + 1) * b], 'row', across)  6.83 us
  transfers between devices with their start and end apart: 49, of which 19 were waited for; matrix products, arithmetic and copies ran while one was open for 4% of the time, Pallas kernels for 24%

profile of v2, /device:TPU:0, one launch (start us, length us, event | category | flops | bytes accessed | tf_op | source)
XLA Modules:
  0.0 235.2 jit_solution(4892330690557471070)
XLA Ops:
  3.1 1.1 broadcast_select_fusion.16
  4.3 3.0 %collective-permute-start.7 = (f32[1024,128]{1,0:T(8,128)S(1)}, f32[1024,128]{1,0:T(8,128)S(1)}, u32[]{:S(2)}, u32[]{:S(2)}) collective-permute-start(f32[1024,128]{1,0:T(8,128)S(1)} %pad_maximum_fusion.4.refs_1_), channel_id=1, source_target_pairs={{0,4},{1,3},{4,8},{5,1},{8,12},{9,5},{12,14},{13,9},{14,10},{15,13... | collective-permute-start | bytes 1572872 | tf_op jit(solution)/shard_map/ppermute | solution.py:265
  7.3 1.6 collective-permute-start.1
  8.9 5.4 %collective-permute-done.7.refs_3_ = f32[1024,128]{1,0:T(8,128)S(1)} collective-permute-done((f32[1024,128]{1,0:T(8,128)S(1)}, f32[1024,128]{1,0:T(8,128)S(1)}, u32[]{:S(2)}, u32[]{:S(2)}) %collective-permute-start.7) | collective-permute-done | bytes 524320 | tf_op jit(solution)/shard_map/ppermute | solution.py:265
  14.4 2.1 collective-permute-start.8
  16.5 3.5 %collective-permute-done.1.refs_2_ = f32[1024,128]{1,0:T(8,128)S(1)} collective-permute-done((f32[1024,128]{1,0:T(8,128)S(1)}, f32[1024,128]{1,0:T(8,128)S(1)}, u32[]{:S(2)}, u32[]{:S(2)}) %collective-permute-start.1) | collective-permute-done | bytes 524320 | tf_op jit(solution)/shard_map/ppermute | solution.py:265
  20.0 2.1 collective-permute-start.2
  22.1 3.6 %collective-permute-done.8.refs_1_ = f32[1024,128]{1,0:T(8,128)} collective-permute-done((f32[1024,128]{1,0:T(8,128)S(1)}, f32[1024,128]{1,0:T(8,128)}, u32[]{:S(2)}, u32[]{:S(2)}) %collective-permute-start.8) | collective-permute-done | bytes 524320 | tf_op jit(solution)/shard_map/ppermute | solution.py:265
  25.7 2.1 collective-permute-start.9
  27.8 3.5 %collective-permute-done.2.refs_0_ = f32[1024,128]{1,0:T(8,128)} collective-permute-done((f32[1024,128]{1,0:T(8,128)S(1)}, f32[1024,128]{1,0:T(8,128)}, u32[]{:S(2)}, u32[]{:S(2)}) %collective-permute-start.2) | collective-permute-done | bytes 524320 | tf_op jit(solution)/shard_map/ppermute | solution.py:265
  31.3 2.1 collective-permute-start.3
  33.9 2.9 %collective-permute-done.9.refs_5_ = f32[1024,128]{1,0:T(8,128)S(1)} collective-permute-done((f32[1024,128]{1,0:T(8,128)}, f32[1024,128]{1,0:T(8,128)S(1)}, u32[]{:S(2)}, u32[]{:S(2)}) %collective-permute-start.9) | collective-permute-done | bytes 524320 | tf_op jit(solution)/shard_map/ppermute | solution.py:265
  36.9 2.1 collective-permute-start.10
  39.0 3.5 %collective-permute-done.3.refs_4_ = f32[1024,128]{1,0:T(8,128)S(1)} collective-permute-done((f32[1024,128]{1,0:T(8,128)}, f32[1024,128]{1,0:T(8,128)S(1)}, u32[]{:S(2)}, u32[]{:S(2)}) %collective-permute-start.3) | collective-permute-done | bytes 524320 | tf_op jit(solution)/shard_map/ppermute | solution.py:265
  42.5 2.1 collective-permute-start.4
  48.2 10.1 %part_product.3 = (f32[256,1024]{1,0:T(8,128)S(1)}, f32[8192,256]{1,0:T(8,128)}) custom-call(s32[3]{0:T(128)S(1)} %pad_add_fusion.2.index_ref, f32[8192,1024]{1,0:T(8,128)} %a_ref.11, f32[1024,128]{1,0:T(8,128)S(1)} %pad_maximum_fusion.2.refs_0_, f32[1024,128]{1,0:T(8,128)S(1)} %pad_maximum_fusion.4.refs_1_, f32[1024,128]{1,0:T(8,128)S(1)} %copy-done.7, ...), custom_call_target="tpu_custom_call" | custom-call | tf_op jit(solution)/shard_map/part_product/pallas_call | solution.py:323
  62.3 11.8 %part_product.4 = (f32[256,1024]{1,0:T(8,128)S(1)}, f32[8192,256]{1,0:T(8,128)}) custom-call(s32[4]{0:T(128)S(1)} %pad_add_fusion.1.index_ref, f32[8192,1024]{1,0:T(8,128)} %a_ref.11, f32[1024,128]{1,0:T(8,128)} %collective-permute-done.2.refs_0_, f32[1024,128]{1,0:T(8,128)} %collective-permute-done.8.refs_1_, ...), custom_call_target="tpu_custom_call", output_to_operand_aliasing={{0}: (10, {}), {1}: (11, {})} | custom-call | tf_op jit(solution)/shard_map/part_product/pallas_call | solution.py:323
  74.1 4.1 %part_product.5 = (f32[256,1024]{1,0:T(8,128)S(1)}, f32[8192,256]{1,0:T(8,128)}) custom-call(s32[1]{0:T(128)} %bitcast.2.index_ref, f32[8192,1024]{1,0:T(8,128)} %a_ref.11, f32[1024,128]{1,0:T(8,128)S(1)} %pad_maximum_fusion.3.refs_0_, f32[1024,128]{1,0:T(8,128)S(1)} %pad_maximum_fusion.5.refs_1_, ...), custom_call_target="tpu_custom_call", output_to_operand_aliasing={{0}: (4, {}), {1}: (5, {})} | custom-call | tf_op jit(solution)/shard_map/part_product/pallas_call | solution.py:323
  78.6 2.1 collective-permute-start.20
  80.7 6.8 %collective-permute-done.20 = f32[128,512]{0,1:T(8,128)S(1)} collective-permute-done((f32[128,512]{0,1:T(8,128)S(1)}, f32[128,512]{0,1:T(8,128)S(1)}, u32[]{:S(2)}, u32[]{:S(2)}) %collective-permute-start.20) | collective-permute-done | bytes 262176 | tf_op jit(solution)/shard_map/ppermute | solution.py:456
  87.6 1.3 collective-permute-start.21
  88.9 5.0 %collective-permute-start.18 = (f32[128,512]{0,1:T(8,128)S(1)}, f32[128,512]{0,1:T(8,128)S(1)}, u32[]{:S(2)}, u32[]{:S(2)}) collective-permute-start(f32[128,512]{0,1:T(8,128)S(1)} %get-tuple-element.28), channel_id=1, source_target_pairs={{0,16},{16,0},{1,17},{17,1},{2,18},{18,2},{3,19},{19,3},{4,20},{20... | collective-permute-start | bytes 786440 | tf_op jit(solution)/shard_map/ppermute | solution.py:456
  93.9 10.1 %collective-permute-done.21 = f32[512,128]{1,0:T(8,128)S(1)} collective-permute-done((f32[512,128]{1,0:T(8,128)S(1)}, f32[512,128]{1,0:T(8,128)S(1)}, u32[]{:S(2)}, u32[]{:S(2)}) %collective-permute-start.21) | collective-permute-done | bytes 262176 | tf_op jit(solution)/shard_map/ppermute | solution.py:467
  104.0 1.3 collective-permute-start.22
  106.1 9.4 %collective-permute-done.22 = f32[512,128]{1,0:T(8,128)S(1)} collective-permute-done((f32[512,128]{1,0:T(8,128)S(1)}, f32[512,128]{1,0:T(8,128)S(1)}, u32[]{:S(2)}, u32[]{:S(2)}) %collective-permute-start.22) | collective-permute-done | bytes 262176 | tf_op jit(solution)/shard_map/ppermute | solution.py:467
  116.2 1.9 own_gram.1
  118.3 3.9 %collective-permute-start.38 = (f32[1024,128]{1,0:T(8,128)S(1)}, f32[1024,128]{1,0:T(8,128)}, u32[]{:S(2)}, u32[]{:S(2)}) collective-permute-start(f32[1024,128]{1,0:T(8,128)S(1)} %pad_maximum_fusion.9.refs_1_), channel_id=1, source_target_pairs={{0,4},{1,3},{4,8},{5,1},{8,12},{9,5},{12,14},{13,9},{14,10},{15,13... | collective-permute-start | bytes 1572872 | tf_op jit(solution)/shard_map/ppermute | solution.py:265
  122.5 2.6 %collective-permute-start.24 = (f32[128,256]{1,0:T(8,128)S(1)}, f32[128,256]{1,0:T(8,128)S(1)}, u32[]{:S(2)}, u32[]{:S(2)}) collective-permute-start(f32[128,256]{1,0:T(8,128)S(1)} %dynamic-slice_add_fusion.2), channel_id=1, source_target_pairs={{0,16},{16,0},{1,17},{17,1},{2,18},{18,2},{3,19},{19,3},{4,20},{20... | collective-permute-start | bytes 393224 | tf_op jit(solution)/shard_map/ppermute | solution.py:427
  125.0 3.9 %collective-permute-done.38.refs_3_ = f32[1024,128]{1,0:T(8,128)} collective-permute-done((f32[1024,128]{1,0:T(8,128)S(1)}, f32[1024,128]{1,0:T(8,128)}, u32[]{:S(2)}, u32[]{:S(2)}) %collective-permute-start.38) | collective-permute-done | bytes 524320 | tf_op jit(solution)/shard_map/ppermute | solution.py:265
  129.0 2.6 %collective-permute-start.39 = (f32[1024,128]{1,0:T(8,128)}, f32[1024,128]{1,0:T(8,128)}, u32[]{:S(2)}, u32[]{:S(2)}) collective-permute-start(f32[1024,128]{1,0:T(8,128)} %collective-permute-done.38.refs_3_), channel_id=1, source_target_pairs={{0,4},{1,3},{4,8},{5,1},{8,12},{9,5},{12,14},{13,9},{14,10},{15,13... | collective-permute-start | bytes 1572872 | tf_op jit(solution)/shard_map/ppermute | solution.py:265
  132.4 2.5 %collective-permute-start.29 = (f32[256,512]{0,1:T(8,128)}, f32[256,512]{0,1:T(8,128)S(1)}, u32[]{:S(2)}, u32[]{:S(2)}) collective-permute-start(f32[256,512]{0,1:T(8,128)} %pad_maximum_fusion.6), channel_id=1, source_target_pairs={{0,16},{16,0},{1,17},{17,1},{2,18},{18,2},{3,19},{19,3},{4,20},{20... | collective-permute-start | bytes 1572872 | tf_op jit(solution)/shard_map/ppermute | solution.py:483
  135.0 6.6 %collective-permute-done.25 = f32[128,256]{1,0:T(8,128)S(1)} collective-permute-done((f32[128,256]{1,0:T(8,128)S(1)}, f32[128,256]{1,0:T(8,128)S(1)}, u32[]{:S(2)}, u32[]{:S(2)}) %collective-permute-start.25) | collective-permute-done | bytes 131104 | tf_op jit(solution)/shard_map/ppermute | solution.py:430
  141.7 2.0 collective-permute-start.33
  143.7 2.2 constant_dynamic-slice_fusion.2
  146.0 6.6 %collective-permute-start.30 = (f32[1024,256]{1,0:T(8,128)}, f32[1024,256]{1,0:T(8,128)}, u32[]{:S(2)}, u32[]{:S(2)}) collective-permute-start(f32[1024,256]{1,0:T(8,128)} %constant_dynamic-slice_fusion.2), channel_id=1, source_target_pairs={{0,16},{1,17},{2,18},{3,19},{4,20},{5,21},{6,22},{7,23},{24,8},{25... | collective-permute-start | bytes 3145736 | tf_op jit(solution)/shard_map/ppermute | solution.py:481
  153.2 8.2 %collective-permute-done.27 = f32[128,256]{1,0:T(8,128)S(1)} collective-permute-done((f32[128,256]{1,0:T(8,128)S(1)}, f32[128,256]{1,0:T(8,128)S(1)}, u32[]{:S(2)}, u32[]{:S(2)}) %collective-permute-start.27) | collective-permute-done | bytes 131104 | tf_op jit(solution)/shard_map/ppermute | solution.py:430
  161.6 2.5 %collective-permute-start.46 = (f32[1024,128]{1,0:T(8,128)}, f32[1024,128]{1,0:T(8,128)}, u32[]{:S(2)}, u32[]{:S(2)}) collective-permute-start(f32[1024,128]{1,0:T(8,128)} %collective-permute-done.38.refs_3_), channel_id=1, source_target_pairs={{0,1},{1,0},{2,3},{3,2},{4,5},{5,4},{6,7},{7,6},{8,9},{9,8},{10,11... | collective-permute-start | bytes 1572872 | tf_op jit(solution)/shard_map/ppermute | solution.py:267
  165.5 1.6 copy.12.zt_ref
  167.1 4.1 %collective-permute-done.40.refs_1_ = f32[1024,128]{1,0:T(8,128)S(1)} collective-permute-done((f32[1024,128]{1,0:T(8,128)}, f32[1024,128]{1,0:T(8,128)S(1)}, u32[]{:S(2)}, u32[]{:S(2)}) %collective-permute-start.40) | collective-permute-done | bytes 524320 | tf_op jit(solution)/shard_map/ppermute | solution.py:265
  171.3 1.6 collective-permute-done.30
  172.8 1.9 collective-permute-start.44
  174.7 2.1 collective-permute-done.34.refs_0_
  176.9 1.4 broadcast_select_fusion
  178.3 2.1 collective-permute-start.35
  180.7 4.4 %factors.1 = (bf16[512,1024]{1,0:T(8,128)(2,1)S(1)}, bf16[512,1024]{1,0:T(8,128)(2,1)S(1)}) custom-call(f32[2,128,128]{2,1,0:T(8,128)S(1)} %copy-done.8, f32[256,256]{1,0:T(8,128)S(1)} %pad_maximum_fusion.11.m_ref, f32[128,128]{1,0:T(8,128)S(1)} %slice.36.n_ref, f32[256,1024]{1,0:T(8,128)S(1)} %copy.12.zt_ref, f32[2,1024,128]{2,1,0:T(8,128)S(1)} %pad_maximum_fusion.1.vc_ref), custom_call_target="tpu_custom_call" | custom-call | tf_op jit(solution)/shard_map/factors/pallas_call | solution.py:149
  187.1 27.7 %part_update.3.refs_4_ = f32[8192,1024]{1,0:T(8,128)} custom-call(s32[10]{0:T(128)S(1)} %stack.127.index_ref, f32[8192,1024]{1,0:T(8,128)} %a_ref.11, f32[8192,256]{1,0:T(8,128)} %get-tuple-element.18.v_ref, bf16[512,1024]{1,0:T(8,128)(2,1)} %copy-done, bf16[512,1024]{1,0:T(8,128)(2,1)} %copy-done.2, f32[1024,128]{1,0:T(8,128)S(1)} %pad_maximum_fusion.7.refs_0_, ...), custom_call_target="tpu_custom_call" | custom-call | tf_op jit(solution)/shard_map/part_update/pallas_call | solution.py:404
  215.3 12.2 %part_update.4.refs_2_ = f32[8192,1024]{1,0:T(8,128)} custom-call(s32[4]{0:T(128)S(1)} %pad_add_fusion.3.index_ref, f32[8192,1024]{1,0:T(8,128)} %a_ref.11, f32[8192,256]{1,0:T(8,128)} %get-tuple-element.18.v_ref, bf16[512,1024]{1,0:T(8,128)(2,1)S(1)} %copy-done.1, bf16[512,1024]{1,0:T(8,128)(2,1)S(1)} %copy-done.3, ...), custom_call_target="tpu_custom_call", output_to_operand_aliasing={{}: (9, {})} | custom-call | tf_op jit(solution)/shard_map/part_update/pallas_call | solution.py:404
  227.7 7.5 %part_update.5 = f32[8192,1024]{1,0:T(8,128)} custom-call(s32[2]{0:T(128)S(1)} %pad_add_fusion.index_ref, f32[8192,1024]{1,0:T(8,128)} %a_ref.11, f32[8192,256]{1,0:T(8,128)} %get-tuple-element.18.v_ref, bf16[512,1024]{1,0:T(8,128)(2,1)S(1)} %copy-done.1, bf16[512,1024]{1,0:T(8,128)(2,1)S(1)} %copy-done.3, ...), custom_call_target="tpu_custom_call", output_to_operand_aliasing={{}: (7, {})} | custom-call | tf_op jit(solution)/shard_map/part_update/pallas_call | solution.py:404
  (124 shorter events, 19.2 us)
Async XLA Ops:
  1.1 1.7 collective-permute-start
  4.3 10.1 %collective-permute-start.7 = (f32[1024,128]{1,0:T(8,128)S(1)}, f32[1024,128]{1,0:T(8,128)S(1)}, u32[]{:S(2)}, u32[]{:S(2)}) collective-permute-start(f32[1024,128]{1,0:T(8,128)S(1)} %pad_maximum_fusion.4.refs_1_), channel_id=1, source_target_pairs={{0,4},{1,3},{4,8},{5,1},{8,12},{9,5},{12,14},{13,9},{14,10},{15,13... | collective-permute-start | bytes 1572872 | tf_op jit(solution)/shard_map/ppermute | solution.py:265
  7.3 12.7 %collective-permute-start.1 = (f32[1024,128]{1,0:T(8,128)S(1)}, f32[1024,128]{1,0:T(8,128)S(1)}, u32[]{:S(2)}, u32[]{:S(2)}) collective-permute-start(f32[1024,128]{1,0:T(8,128)S(1)} %pad_maximum_fusion.2.refs_0_), channel_id=1, source_target_pairs={{0,4},{1,3},{4,8},{5,1},{8,12},{9,5},{12,14},{13,9},{14,10},{15,13... | collective-permute-start | bytes 1572872 | tf_op jit(solution)/shard_map/ppermute | solution.py:265
  14.4 11.3 %collective-permute-start.8 = (f32[1024,128]{1,0:T(8,128)S(1)}, f32[1024,128]{1,0:T(8,128)}, u32[]{:S(2)}, u32[]{:S(2)}) collective-permute-start(f32[1024,128]{1,0:T(8,128)S(1)} %collective-permute-done.7.refs_3_), channel_id=1, source_target_pairs={{0,4},{1,3},{4,8},{5,1},{8,12},{9,5},{12,14},{13,9},{14,10},{15,13... | collective-permute-start | bytes 1572872 | tf_op jit(solution)/shard_map/ppermute | solution.py:265
  20.0 11.3 %collective-permute-start.2 = (f32[1024,128]{1,0:T(8,128)S(1)}, f32[1024,128]{1,0:T(8,128)}, u32[]{:S(2)}, u32[]{:S(2)}) collective-permute-start(f32[1024,128]{1,0:T(8,128)S(1)} %collective-permute-done.1.refs_2_), channel_id=1, source_target_pairs={{0,4},{1,3},{4,8},{5,1},{8,12},{9,5},{12,14},{13,9},{14,10},{15,13... | collective-permute-start | bytes 1572872 | tf_op jit(solution)/shard_map/ppermute | solution.py:265
  25.7 11.1 %collective-permute-start.9 = (f32[1024,128]{1,0:T(8,128)}, f32[1024,128]{1,0:T(8,128)S(1)}, u32[]{:S(2)}, u32[]{:S(2)}) collective-permute-start(f32[1024,128]{1,0:T(8,128)} %collective-permute-done.8.refs_1_), channel_id=1, source_target_pairs={{0,4},{1,3},{4,8},{5,1},{8,12},{9,5},{12,14},{13,9},{14,10},{15,13... | collective-permute-start | bytes 1572872 | tf_op jit(solution)/shard_map/ppermute | solution.py:265
  31.3 11.1 %collective-permute-start.3 = (f32[1024,128]{1,0:T(8,128)}, f32[1024,128]{1,0:T(8,128)S(1)}, u32[]{:S(2)}, u32[]{:S(2)}) collective-permute-start(f32[1024,128]{1,0:T(8,128)} %collective-permute-done.2.refs_0_), channel_id=1, source_target_pairs={{0,4},{1,3},{4,8},{5,1},{8,12},{9,5},{12,14},{13,9},{14,10},{15,13... | collective-permute-start | bytes 1572872 | tf_op jit(solution)/shard_map/ppermute | solution.py:265
  33.4 12.6 %collective-permute-start.17 = (f32[1024,128]{1,0:T(8,128)S(1)}, f32[1024,128]{1,0:T(8,128)}, u32[]{:S(2)}, u32[]{:S(2)}) collective-permute-start(f32[1024,128]{1,0:T(8,128)S(1)} %collective-permute-done.7.refs_3_), channel_id=1, source_target_pairs={{0,1},{1,0},{2,3},{3,2},{4,5},{5,4},{6,7},{7,6},{8,9},{9,8},{10,11... | collective-permute-start | bytes 1572872 | tf_op jit(solution)/shard_map/ppermute | solution.py:267
  33.4 12.7 %collective-permute-start.16 = (f32[1024,128]{1,0:T(8,128)S(1)}, f32[1024,128]{1,0:T(8,128)}, u32[]{:S(2)}, u32[]{:S(2)}) collective-permute-start(f32[1024,128]{1,0:T(8,128)S(1)} %collective-permute-done.1.refs_2_), channel_id=1, source_target_pairs={{0,1},{1,0},{2,3},{3,2},{4,5},{5,4},{6,7},{7,6},{8,9},{9,8},{10,11... | collective-permute-start | bytes 1572872 | tf_op jit(solution)/shard_map/ppermute | solution.py:267
  36.9 8.5 %collective-permute-start.10 = (f32[512,128]{1,0:T(8,128)S(1)}, f32[512,128]{1,0:T(8,128)}, u32[]{:S(2)}, u32[]{:S(2)}) collective-permute-start(f32[512,128]{1,0:T(8,128)S(1)} %constant_dynamic-slice_fusion.5), channel_id=1, source_target_pairs={{0,4},{1,3},{4,8},{5,1},{8,12},{9,5},{12,14},{13,9},{14,10},{15,13... | collective-permute-start | bytes 786440 | tf_op jit(solution)/shard_map/ppermute | solution.py:271
  42.5 16.2 %collective-permute-start.4 = (f32[512,128]{1,0:T(8,128)S(1)}, f32[512,128]{1,0:T(8,128)}, u32[]{:S(2)}, u32[]{:S(2)}) collective-permute-start(f32[512,128]{1,0:T(8,128)S(1)} %constant_dynamic-slice_fusion.6), channel_id=1, source_target_pairs={{0,4},{1,3},{4,8},{5,1},{8,12},{9,5},{12,14},{13,9},{14,10},{15,13... | collective-permute-start | bytes 786440 | tf_op jit(solution)/shard_map/ppermute | solution.py:271
  45.4 13.4 %collective-permute-start.11 = (f32[512,128]{1,0:T(8,128)}, f32[512,128]{1,0:T(8,128)}, u32[]{:S(2)}, u32[]{:S(2)}) collective-permute-start(f32[512,128]{1,0:T(8,128)} %collective-permute-done.10), channel_id=1, source_target_pairs={{0,1},{1,0},{2,3},{3,2},{4,5},{5,4},{6,7},{7,6},{8,9},{9,8},{10,11... | collective-permute-start | bytes 786440 | tf_op jit(solution)/shard_map/ppermute | solution.py:258
  45.5 16.7 %collective-permute-start.13 = (f32[1024,128]{1,0:T(8,128)}, f32[1024,128]{1,0:T(8,128)S(1)}, u32[]{:S(2)}, u32[]{:S(2)}) collective-permute-start(f32[1024,128]{1,0:T(8,128)} %collective-permute-done.8.refs_1_), channel_id=1, source_target_pairs={{0,1},{1,0},{2,3},{3,2},{4,5},{5,4},{6,7},{7,6},{8,9},{9,8},{10,11... | collective-permute-start | bytes 1572872 | tf_op jit(solution)/shard_map/ppermute | solution.py:267
  46.0 16.2 %collective-permute-start.12 = (f32[1024,128]{1,0:T(8,128)}, f32[1024,128]{1,0:T(8,128)S(1)}, u32[]{:S(2)}, u32[]{:S(2)}) collective-permute-start(f32[1024,128]{1,0:T(8,128)} %collective-permute-done.2.refs_0_), channel_id=1, source_target_pairs={{0,1},{1,0},{2,3},{3,2},{4,5},{5,4},{6,7},{7,6},{8,9},{9,8},{10,11... | collective-permute-start | bytes 1572872 | tf_op jit(solution)/shard_map/ppermute | solution.py:267
  58.3 4.0 %collective-permute-start.15 = (f32[1024,128]{1,0:T(8,128)S(1)}, f32[1024,128]{1,0:T(8,128)S(1)}, u32[]{:S(2)}, u32[]{:S(2)}) collective-permute-start(f32[1024,128]{1,0:T(8,128)S(1)} %collective-permute-done.9.refs_5_), channel_id=1, source_target_pairs={{0,1},{1,0},{2,3},{3,2},{4,5},{5,4},{6,7},{7,6},{8,9},{9,8},{10,11... | collective-permute-start | bytes 1572872 | tf_op jit(solution)/shard_map/ppermute | solution.py:267
  58.7 3.6 %collective-permute-start.14 = (f32[1024,128]{1,0:T(8,128)S(1)}, f32[1024,128]{1,0:T(8,128)S(1)}, u32[]{:S(2)}, u32[]{:S(2)}) collective-permute-start(f32[1024,128]{1,0:T(8,128)S(1)} %collective-permute-done.3.refs_4_), channel_id=1, source_target_pairs={{0,1},{1,0},{2,3},{3,2},{4,5},{5,4},{6,7},{7,6},{8,9},{9,8},{10,11... | collective-permute-start | bytes 1572872 | tf_op jit(solution)/shard_map/ppermute | solution.py:267
  58.8 2.4 %collective-permute-start.5 = (f32[512,128]{1,0:T(8,128)}, f32[512,128]{1,0:T(8,128)S(1)}, u32[]{:S(2)}, u32[]{:S(2)}) collective-permute-start(f32[512,128]{1,0:T(8,128)} %collective-permute-done.4), channel_id=1, source_target_pairs={{0,1},{1,0},{2,3},{3,2},{4,5},{5,4},{6,7},{7,6},{8,9},{9,8},{10,11... | collective-permute-start | bytes 786440 | tf_op jit(solution)/shard_map/ppermute | solution.py:258
  78.6 8.9 %collective-permute-start.20 = (f32[128,512]{0,1:T(8,128)S(1)}, f32[128,512]{0,1:T(8,128)S(1)}, u32[]{:S(2)}, u32[]{:S(2)}) collective-permute-start(f32[128,512]{0,1:T(8,128)S(1)} %dynamic-slice.3), channel_id=1, source_target_pairs={{0,16},{16,0},{1,17},{17,1},{2,18},{18,2},{3,19},{19,3},{4,20},{20... | collective-permute-start | bytes 786440 | tf_op jit(solution)/shard_map/ppermute | solution.py:456
  87.6 16.5 %collective-permute-start.21 = (f32[512,128]{1,0:T(8,128)S(1)}, f32[512,128]{1,0:T(8,128)S(1)}, u32[]{:S(2)}, u32[]{:S(2)}) collective-permute-start(f32[512,128]{1,0:T(8,128)S(1)} %bitcast.45), channel_id=1, source_target_pairs={{8,0},{9,1},{10,2},{11,3},{12,4},{13,5},{14,6},{15,7},{16,24},{17,... | collective-permute-start | bytes 786440 | tf_op jit(solution)/shard_map/ppermute | solution.py:467
  88.9 16.5 %collective-permute-start.18 = (f32[128,512]{0,1:T(8,128)S(1)}, f32[128,512]{0,1:T(8,128)S(1)}, u32[]{:S(2)}, u32[]{:S(2)}) collective-permute-start(f32[128,512]{0,1:T(8,128)S(1)} %get-tuple-element.28), channel_id=1, source_target_pairs={{0,16},{16,0},{1,17},{17,1},{2,18},{18,2},{3,19},{19,3},{4,20},{20... | collective-permute-start | bytes 786440 | tf_op jit(solution)/shard_map/ppermute | solution.py:456
  104.0 11.5 %collective-permute-start.22 = (f32[512,128]{1,0:T(8,128)S(1)}, f32[512,128]{1,0:T(8,128)S(1)}, u32[]{:S(2)}, u32[]{:S(2)}) collective-permute-start(f32[512,128]{1,0:T(8,128)S(1)} %collective-permute-done.21), channel_id=1, source_target_pairs={{0,16},{1,17},{2,18},{3,19},{4,20},{5,21},{6,22},{7,23},{24,8},{25... | collective-permute-start | bytes 786440 | tf_op jit(solution)/shard_map/ppermute | solution.py:467
  105.4 10.2 %collective-permute-start.19 = (f32[512,128]{1,0:T(8,128)S(1)}, f32[512,128]{1,0:T(8,128)S(1)}, u32[]{:S(2)}, u32[]{:S(2)}) collective-permute-start(f32[512,128]{1,0:T(8,128)S(1)} %bitcast.46), channel_id=1, source_target_pairs={{8,16},{9,17},{10,18},{11,19},{12,20},{13,21},{14,22},{15,23},{16,... | collective-permute-start | bytes 786440 | tf_op jit(solution)/shard_map/ppermute | solution.py:466
  115.5 2.7 %collective-permute-start.37 = (f32[512,128]{1,0:T(8,128)S(1)}, f32[512,128]{1,0:T(8,128)S(1)}, u32[]{:S(2)}, u32[]{:S(2)}) collective-permute-start(f32[512,128]{1,0:T(8,128)S(1)} %broadcast_select_fusion.3.z2_ref), channel_id=1, source_target_pairs={{0,1},{1,0},{2,3},{3,2},{4,5},{5,4},{6,7},{7,6},{8,9},{9,8},{10,11... | collective-permute-start | bytes 786440 | tf_op jit(solution)/shard_map/ppermute | solution.py:258
  115.7 6.6 %collective-permute-start.31 = (f32[512,128]{1,0:T(8,128)S(1)}, f32[512,128]{1,0:T(8,128)S(1)}, u32[]{:S(2)}, u32[]{:S(2)}) collective-permute-start(f32[512,128]{1,0:T(8,128)S(1)} %broadcast_select_fusion.4.z1_ref), channel_id=1, source_target_pairs={{0,1},{1,0},{2,3},{3,2},{4,5},{5,4},{6,7},{7,6},{8,9},{9,8},{10,11... | collective-permute-start | bytes 786440 | tf_op jit(solution)/shard_map/ppermute | solution.py:258
  118.2 4.3 %collective-permute-start.23 = (f32[128,256]{1,0:T(8,128)S(1)}, f32[128,256]{1,0:T(8,128)S(1)}, u32[]{:S(2)}, u32[]{:S(2)}) collective-permute-start(f32[128,256]{1,0:T(8,128)S(1)} %constant_dynamic-slice_fusion.3), channel_id=1, source_target_pairs={{0,1},{1,0},{2,3},{3,2},{4,5},{5,4},{6,7},{7,6},{8,9},{9,8},{10,11... | collective-permute-start | bytes 393224 | tf_op jit(solution)/shard_map/ppermute | solution.py:426
  118.3 10.6 %collective-permute-start.38 = (f32[1024,128]{1,0:T(8,128)S(1)}, f32[1024,128]{1,0:T(8,128)}, u32[]{:S(2)}, u32[]{:S(2)}) collective-permute-start(f32[1024,128]{1,0:T(8,128)S(1)} %pad_maximum_fusion.9.refs_1_), channel_id=1, source_target_pairs={{0,4},{1,3},{4,8},{5,1},{8,12},{9,5},{12,14},{13,9},{14,10},{15,13... | collective-permute-start | bytes 1572872 | tf_op jit(solution)/shard_map/ppermute | solution.py:265
  122.4 19.4 %collective-permute-start.32 = (f32[1024,128]{1,0:T(8,128)S(1)}, f32[1024,128]{1,0:T(8,128)}, u32[]{:S(2)}, u32[]{:S(2)}) collective-permute-start(f32[1024,128]{1,0:T(8,128)S(1)} %pad_maximum_fusion.7.refs_0_), channel_id=1, source_target_pairs={{0,4},{1,3},{4,8},{5,1},{8,12},{9,5},{12,14},{13,9},{14,10},{15,13... | collective-permute-start | bytes 1572872 | tf_op jit(solution)/shard_map/ppermute | solution.py:265
  122.5 12.4 %collective-permute-start.24 = (f32[128,256]{1,0:T(8,128)S(1)}, f32[128,256]{1,0:T(8,128)S(1)}, u32[]{:S(2)}, u32[]{:S(2)}) collective-permute-start(f32[128,256]{1,0:T(8,128)S(1)} %dynamic-slice_add_fusion.2), channel_id=1, source_target_pairs={{0,16},{16,0},{1,17},{17,1},{2,18},{18,2},{3,19},{19,3},{4,20},{20... | collective-permute-start | bytes 393224 | tf_op jit(solution)/shard_map/ppermute | solution.py:427
  129.0 32.5 %collective-permute-start.39 = (f32[1024,128]{1,0:T(8,128)}, f32[1024,128]{1,0:T(8,128)}, u32[]{:S(2)}, u32[]{:S(2)}) collective-permute-start(f32[1024,128]{1,0:T(8,128)} %collective-permute-done.38.refs_3_), channel_id=1, source_target_pairs={{0,4},{1,3},{4,8},{5,1},{8,12},{9,5},{12,14},{13,9},{14,10},{15,13... | collective-permute-start | bytes 1572872 | tf_op jit(solution)/shard_map/ppermute | solution.py:265
  132.4 29.1 %collective-permute-start.29 = (f32[256,512]{0,1:T(8,128)}, f32[256,512]{0,1:T(8,128)S(1)}, u32[]{:S(2)}, u32[]{:S(2)}) collective-permute-start(f32[256,512]{0,1:T(8,128)} %pad_maximum_fusion.6), channel_id=1, source_target_pairs={{0,16},{16,0},{1,17},{17,1},{2,18},{18,2},{3,19},{19,3},{4,20},{20... | collective-permute-start | bytes 1572872 | tf_op jit(solution)/shard_map/ppermute | solution.py:483
  134.9 6.7 %collective-permute-start.25 = (f32[128,256]{1,0:T(8,128)S(1)}, f32[128,256]{1,0:T(8,128)S(1)}, u32[]{:S(2)}, u32[]{:S(2)}) collective-permute-start(f32[128,256]{1,0:T(8,128)S(1)} %add.276), channel_id=1, source_target_pairs={{0,2},{1,3},{2,0},{3,1},{4,6},{5,7},{6,4},{7,5},{8,10},{9,11},{10,... | collective-permute-start | bytes 393224 | tf_op jit(solution)/shard_map/ppermute | solution.py:430
  141.6 10.9 %collective-permute-start.26 = (f32[128,256]{1,0:T(8,128)S(1)}, f32[128,256]{1,0:T(8,128)S(1)}, u32[]{:S(2)}, u32[]{:S(2)}) collective-permute-start(f32[128,256]{1,0:T(8,128)S(1)} %add.277), channel_id=1, source_target_pairs={{0,4},{1,5},{2,6},{3,7},{4,0},{5,1},{6,2},{7,3},{8,12},{9,13},{10,... | collective-permute-start | bytes 393224 | tf_op jit(solution)/shard_map/ppermute | solution.py:430
  141.7 22.5 %collective-permute-start.33 = (f32[1024,128]{1,0:T(8,128)}, f32[1024,128]{1,0:T(8,128)}, u32[]{:S(2)}, u32[]{:S(2)}) collective-permute-start(f32[1024,128]{1,0:T(8,128)} %collective-permute-done.32.refs_2_), channel_id=1, source_target_pairs={{0,4},{1,3},{4,8},{5,1},{8,12},{9,5},{12,14},{13,9},{14,10},{15,13... | collective-permute-start | bytes 1572872 | tf_op jit(solution)/shard_map/ppermute | solution.py:265
  146.0 26.8 %collective-permute-start.30 = (f32[1024,256]{1,0:T(8,128)}, f32[1024,256]{1,0:T(8,128)}, u32[]{:S(2)}, u32[]{:S(2)}) collective-permute-start(f32[1024,256]{1,0:T(8,128)} %constant_dynamic-slice_fusion.2), channel_id=1, source_target_pairs={{0,16},{1,17},{2,18},{3,19},{4,20},{5,21},{6,22},{7,23},{24,8},{25... | collective-permute-start | bytes 3145736 | tf_op jit(solution)/shard_map/ppermute | solution.py:481
  152.6 8.7 %collective-permute-start.27 = (f32[128,256]{1,0:T(8,128)S(1)}, f32[128,256]{1,0:T(8,128)S(1)}, u32[]{:S(2)}, u32[]{:S(2)}) collective-permute-start(f32[128,256]{1,0:T(8,128)S(1)} %add.278), channel_id=1, source_target_pairs={{0,8},{1,9},{2,10},{3,11},{4,12},{5,13},{6,14},{7,15},{8,0},{9,1},... | collective-permute-start | bytes 393224 | tf_op jit(solution)/shard_map/ppermute | solution.py:430
  161.4 2.8 %collective-permute-start.28 = (f32[128,256]{1,0:T(8,128)S(1)}, f32[128,256]{1,0:T(8,128)S(1)}, u32[]{:S(2)}, u32[]{:S(2)}) collective-permute-start(f32[128,256]{1,0:T(8,128)S(1)} %add.279), channel_id=1, source_target_pairs={{0,1},{1,0},{2,3},{3,2},{4,5},{5,4},{6,7},{7,6},{8,9},{9,8},{10,11... | collective-permute-start | bytes 393224 | tf_op jit(solution)/shard_map/ppermute | solution.py:432
  161.5 9.8 %collective-permute-start.40 = (f32[1024,128]{1,0:T(8,128)}, f32[1024,128]{1,0:T(8,128)S(1)}, u32[]{:S(2)}, u32[]{:S(2)}) collective-permute-start(f32[1024,128]{1,0:T(8,128)} %collective-permute-done.39.refs_7_), channel_id=1, source_target_pairs={{0,4},{1,3},{4,8},{5,1},{8,12},{9,5},{12,14},{13,9},{14,10},{15,13... | collective-permute-start | bytes 1572872 | tf_op jit(solution)/shard_map/ppermute | solution.py:265
  161.6 11.2 %collective-permute-start.46 = (f32[1024,128]{1,0:T(8,128)}, f32[1024,128]{1,0:T(8,128)}, u32[]{:S(2)}, u32[]{:S(2)}) collective-permute-start(f32[1024,128]{1,0:T(8,128)} %collective-permute-done.38.refs_3_), channel_id=1, source_target_pairs={{0,1},{1,0},{2,3},{3,2},{4,5},{5,4},{6,7},{7,6},{8,9},{9,8},{10,11... | collective-permute-start | bytes 1572872 | tf_op jit(solution)/shard_map/ppermute | solution.py:267
  164.2 8.7 %collective-permute-start.45 = (f32[1024,128]{1,0:T(8,128)}, f32[1024,128]{1,0:T(8,128)}, u32[]{:S(2)}, u32[]{:S(2)}) collective-permute-start(f32[1024,128]{1,0:T(8,128)} %collective-permute-done.32.refs_2_), channel_id=1, source_target_pairs={{0,1},{1,0},{2,3},{3,2},{4,5},{5,4},{6,7},{7,6},{8,9},{9,8},{10,11... | collective-permute-start | bytes 1572872 | tf_op jit(solution)/shard_map/ppermute | solution.py:267
  164.3 12.6 %collective-permute-start.34 = (f32[1024,128]{1,0:T(8,128)}, f32[1024,128]{1,0:T(8,128)S(1)}, u32[]{:S(2)}, u32[]{:S(2)}) collective-permute-start(f32[1024,128]{1,0:T(8,128)} %collective-permute-done.33.refs_6_), channel_id=1, source_target_pairs={{0,4},{1,3},{4,8},{5,1},{8,12},{9,5},{12,14},{13,9},{14,10},{15,13... | collective-permute-start | bytes 1572872 | tf_op jit(solution)/shard_map/ppermute | solution.py:265
  171.2 7.0 %collective-permute-start.48 = (f32[1024,128]{1,0:T(8,128)}, f32[1024,128]{1,0:T(8,128)S(1)}, u32[]{:S(2)}, u32[]{:S(2)}) collective-permute-start(f32[1024,128]{1,0:T(8,128)} %collective-permute-done.39.refs_7_), channel_id=1, source_target_pairs={{0,1},{1,0},{2,3},{3,2},{4,5},{5,4},{6,7},{7,6},{8,9},{9,8},{10,11... | collective-permute-start | bytes 1572872 | tf_op jit(solution)/shard_map/ppermute | solution.py:267
  172.8 14.3 %collective-permute-start.47 = (f32[1024,128]{1,0:T(8,128)}, f32[1024,128]{1,0:T(8,128)S(1)}, u32[]{:S(2)}, u32[]{:S(2)}) collective-permute-start(f32[1024,128]{1,0:T(8,128)} %collective-permute-done.33.refs_6_), channel_id=1, source_target_pairs={{0,1},{1,0},{2,3},{3,2},{4,5},{5,4},{6,7},{7,6},{8,9},{9,8},{10,11... | collective-permute-start | bytes 1572872 | tf_op jit(solution)/shard_map/ppermute | solution.py:267
  172.8 7.6 %collective-permute-start.41 = (f32[512,128]{1,0:T(8,128)S(1)}, f32[512,128]{1,0:T(8,128)S(1)}, u32[]{:S(2)}, u32[]{:S(2)}) collective-permute-start(f32[512,128]{1,0:T(8,128)S(1)} %constant_dynamic-slice_fusion), channel_id=1, source_target_pairs={{0,4},{1,3},{4,8},{5,1},{8,12},{9,5},{12,14},{13,9},{14,10},{15,13... | collective-permute-start | bytes 786440 | tf_op jit(solution)/shard_map/ppermute | solution.py:271
  172.8 42.4 %collective-permute-start.44 = (f32[1024,128]{1,0:T(8,128)S(1)}, f32[1024,128]{1,0:T(8,128)S(1)}, u32[]{:S(2)}, u32[]{:S(2)}) collective-permute-start(f32[1024,128]{1,0:T(8,128)S(1)} %collective-permute-done.40.refs_1_), channel_id=1, source_target_pairs={{0,1},{1,0},{2,3},{3,2},{4,5},{5,4},{6,7},{7,6},{8,9},{9,8},{10,11... | collective-permute-start | bytes 1572872 | tf_op jit(solution)/shard_map/ppermute | solution.py:267
  176.9 38.4 %collective-permute-start.43 = (f32[1024,128]{1,0:T(8,128)S(1)}, f32[1024,128]{1,0:T(8,128)S(1)}, u32[]{:S(2)}, u32[]{:S(2)}) collective-permute-start(f32[1024,128]{1,0:T(8,128)S(1)} %collective-permute-done.34.refs_0_), channel_id=1, source_target_pairs={{0,1},{1,0},{2,3},{3,2},{4,5},{5,4},{6,7},{7,6},{8,9},{9,8},{10,11... | collective-permute-start | bytes 1572872 | tf_op jit(solution)/shard_map/ppermute | solution.py:267
  178.3 36.6 %collective-permute-start.35 = (f32[512,128]{1,0:T(8,128)S(1)}, f32[512,128]{1,0:T(8,128)S(1)}, u32[]{:S(2)}, u32[]{:S(2)}) collective-permute-start(f32[512,128]{1,0:T(8,128)S(1)} %constant_dynamic-slice_fusion.1), channel_id=1, source_target_pairs={{0,4},{1,3},{4,8},{5,1},{8,12},{9,5},{12,14},{13,9},{14,10},{15,13... | collective-permute-start | bytes 786440 | tf_op jit(solution)/shard_map/ppermute | solution.py:271
  180.4 47.1 %collective-permute-start.42 = (f32[512,128]{1,0:T(8,128)S(1)}, f32[512,128]{1,0:T(8,128)S(1)}, u32[]{:S(2)}, u32[]{:S(2)}) collective-permute-start(f32[512,128]{1,0:T(8,128)S(1)} %collective-permute-done.41), channel_id=1, source_target_pairs={{0,1},{1,0},{2,3},{3,2},{4,5},{5,4},{6,7},{7,6},{8,9},{9,8},{10,11... | collective-permute-start | bytes 786440 | tf_op jit(solution)/shard_map/ppermute | solution.py:258
  214.9 12.7 %collective-permute-start.36 = (f32[512,128]{1,0:T(8,128)S(1)}, f32[512,128]{1,0:T(8,128)S(1)}, u32[]{:S(2)}, u32[]{:S(2)}) collective-permute-start(f32[512,128]{1,0:T(8,128)S(1)} %collective-permute-done.35), channel_id=1, source_target_pairs={{0,1},{1,0},{2,3},{3,2},{4,5},{5,4},{6,7},{7,6},{8,9},{9,8},{10,11... | collective-permute-start | bytes 786440 | tf_op jit(solution)/shard_map/ppermute | solution.py:258
  (10 other events, 226.4 us)

commit v3 on v2

--- a/solution.py
+++ b/solution.py
@@ -29,6 +29,10 @@
 
 def exact_nt(left, right):
     return lax.dot_general(left, right, (((1,), (1,)), ((), ())), precision=highest, preferred_element_type=f32)
+
+
+def cost(flops, count):
+    return pl.CostEstimate(flops=flops, bytes_accessed=count, transcendentals=0)
 
 
 def row_block(rows):
@@ -272,6 +276,53 @@
     return result
 
 
+def after(value, *others):
+    if not others:
+        return value
+    vmem = pl.BlockSpec(memory_space=pltpu.VMEM)
+
+    def kernel(*refs):
+        refs[-1][...] = refs[0][...]
+
+    return pl.pallas_call(
+        kernel,
+        in_specs=[vmem] * (1 + len(others)),
+        out_specs=vmem,
+        out_shape=jax.ShapeDtypeStruct(value.shape, value.dtype),
+        compiler_params=pltpu.CompilerParams(vmem_limit_bytes=VMEM_LIMIT),
+        name="after",
+    )(value, *others)
+
+
+def chip_block(mine):
+    core = lax.axis_index("col") % 2
+    other = lax.ppermute(mine, "col", [(c, c ^ 1) for c in range(lax.axis_size("col"))])
+    first, second = jnp.where(core == 0, mine, other), jnp.where(core == 0, other, mine)
+    return jnp.concatenate([first, second], axis=0)
+
+
+def ring_work(own_block, work):
+    chips = lax.axis_size("col") // 2
+    core = lax.axis_index("col") % 2
+    swap = [(c, c ^ 1) for c in range(2 * chips)]
+    around = []
+    for i in range(chips):
+        around.append((2 * ring_chip(i, chips), 2 * ring_chip(i + 1, chips)))
+        around.append((2 * ring_chip(i, chips) + 1, 2 * ring_chip(i - 1, chips) + 1))
+
+    held = own_block
+    blocks = [held]
+    for step in range(1, chips // 2 + 1):
+        if step == chips // 2:
+            rows = held.shape[0] // 2
+            held = lax.dynamic_slice_in_dim(held, core * rows, rows, 0)
+        came = lax.ppermute(held, "col", around)
+        held = after(came, *work(step - 1, blocks))
+        if step < chips // 2:
+            blocks = [held, lax.ppermute(held, "col", swap)]
+    work(chips // 2, [chip_block(held)])
+
+
 def ring_order(chips):
     came, other = ring_chips_here(chips, range(chips // 2 + 1))
     order = [came[0]]
@@ -281,55 +332,64 @@
 
 
 def part_kernel(count, first, index_ref, a_ref, *refs):
-    values, refs = refs[: 2 * count], refs[2 * count :]
+    values, refs = refs[:count], refs[count:]
     if first:
-        out_ref, v_ref = refs
+        out_ref, v_ref, cross_ref = refs
     else:
-        total_ref, _, out_ref, v_ref = refs
+        total_ref, _, sum_ref, out_ref, v_ref, cross_ref = refs
     step = pl.program_id(0)
 
     @pl.when(step == 0)
     def _():
         out_ref[...] = jnp.zeros_like(out_ref) if first else total_ref[...]
+        cross_ref[...] = jnp.zeros_like(cross_ref) if first else sum_ref[...]
 
     for j in range(count):
 
         @pl.when(step == j)
         def _(j=j):
-            v_ref[...] = jnp.concatenate([values[2 * j][...], values[2 * j + 1][...]], axis=1)
+            v_ref[...] = values[j][...]
 
     v_hi, v_lo = split(v_ref[...].T)
     a_hi, a_lo = split(a_ref[...])
     wide = v_hi.shape[0]
     both = dot(jnp.concatenate([v_hi, v_lo], axis=0), a_hi)
     out_ref[...] += both[:wide] + (both[wide:] + dot(v_hi, a_lo))
+    b = wide // 2
+    w_hi, w_lo = split(v_ref[:, b:])
+    cross_ref[...] += dot(v_hi[:b], w_hi) + (dot(v_lo[:b], w_hi) + dot(v_hi[:b], w_lo))
 
 
 def part_product(a, blocks, index, state):
     rows, cols = a.shape
-    block, b = blocks[0][0].shape
+    block, wide = blocks[0].shape
     count = len(blocks)
     first = state is None
-    wide = 2 * b
-    whole = pl.BlockSpec((block, b), lambda i, index: (0, 0))
+    whole = pl.BlockSpec(memory_space=pltpu.VMEM)
     total = pl.BlockSpec((wide, cols), lambda i, index: (0, 0))
-    in_specs = [pl.BlockSpec((block, cols), lambda i, index: (index[i], 0))] + [whole] * (2 * count)
-    operands = [value for pair in blocks for value in pair]
+    in_specs = [pl.BlockSpec((block, cols), lambda i, index: (index[i], 0))] + [whole] * count
+    operands = list(blocks)
     aliases = {}
+    cross = pl.BlockSpec((wide // 2, wide // 2), lambda i, index: (0, 0))
     if not first:
-        in_specs += [total, pl.BlockSpec(memory_space=pl.ANY)]
+        in_specs += [total, pl.BlockSpec(memory_space=pl.ANY), cross]
         operands += list(state)
-        aliases = {2 + 2 * count: 0, 3 + 2 * count: 1}
+        aliases = {2 + count: 0, 3 + count: 1}
     return pl.pallas_call(
         functools.partial(part_kernel, count, first),
         grid_spec=pltpu.PrefetchScalarGridSpec(
             num_scalar_prefetch=1,
             grid=(count,),
             in_specs=in_specs,
-            out_specs=[total, pl.BlockSpec((block, wide), lambda i, index: (index[i], 0))],
+            out_specs=[total, pl.BlockSpec((block, wide), lambda i, index: (index[i], 0)), cross],
         ),
-        out_shape=(jax.ShapeDtypeStruct((wide, cols), f32), jax.ShapeDtypeStruct((rows, wide), f32)),
+        out_shape=(
+            jax.ShapeDtypeStruct((wide, cols), f32),
+            jax.ShapeDtypeStruct((rows, wide), f32),
+            jax.ShapeDtypeStruct((wide // 2, wide // 2), f32),
+        ),
         input_output_aliases=aliases,
+        cost_estimate=cost(6 * count * block * cols * wide, 4 * count * block * (cols + 2 * wide)),
         compiler_params=pltpu.CompilerParams(vmem_limit_bytes=VMEM_LIMIT),
         name="part_product",
     )(index, a, *operands)
@@ -444,11 +504,16 @@
     both = ("row", "col")
 
     order = ring_order(chips)
-    v_blocks = list(zip(*ring_gather([vectors[0], vectors[1]])))
     state = None
-    for begin, end in ((0, 3), (3, chips - 1), (chips - 1, chips)):
-        state = part_product(matrix, v_blocks[begin:end], jnp.stack(order[begin:end]).astype(jnp.int32), state)
-    part, v_rows = state
+
+    def multiply(step, blocks):
+        nonlocal state
+        here = order[:1] if step == 0 else order[2 * step - 1 : 2 * step + 1]
+        state = part_product(matrix, blocks, jnp.stack(here).astype(jnp.int32), state)
+        return [state[2]]
+
+    ring_work(chip_block(jnp.concatenate([vectors[0], vectors[1]], axis=1)), multiply)
+    part, v_rows, _ = state
 
     keep = lax.dynamic_slice_in_dim(part, row * own, own, 1)
     give = lax.dynamic_slice_in_dim(part, (1 - row) * own, own, 1)
@@ -486,11 +551,8 @@
     z_blocks = list(zip(*ring_gather([z1, z2])))
     v_pair = jnp.stack([v_cols[:, :b], v_cols[:, b:]])
     hi, lo = factors(tfactor, small, small[b:, :b], zt, v_pair)
-    out = None
-    for begin, end in ((0, chips - 3), (chips - 3, chips - 1), (chips - 1, chips)):
-        index = jnp.stack([z_index(j, k) for j in order[begin:end] for k in range(2)]).astype(jnp.int32)
-        out = part_update(matrix, v_rows, hi, lo, z_blocks[begin:end], index, out)
-    return out
+    index = jnp.stack([z_index(j, k) for j in order for k in range(2)]).astype(jnp.int32)
+    return part_update(matrix, v_rows, hi, lo, z_blocks, index, None)
 
 
 def solution(mesh):

time: 236 us -> 243 us (1.030); the launches traced: 235 us -> 239 us
  Pallas kernels: 79.8 us -> 96 us
  starting transfers between devices: 58.9 us -> 45.8 us
  waiting for transfers between devices: 78.6 us -> 81.3 us
    ppermute x12 -> x6, waiting for transfers between devices: 32.7 us -> 6.6 us  [ring_gather(): held = [lax.ppermute(block, 'col', around) for block in held]]
    ppermute x0 -> x9, waiting for transfers between devices: none -> 21.7 us  [the longest x4 17.5 us: ring_work(): came = lax.ppermute(held, 'col', around)]
    ppermute x12 -> x6, starting transfers between devices: 21.8 us -> 4.93 us  [ring_gather(): held = [lax.ppermute(block, 'col', around) for block in held]]
    ppermute x0 -> x9, starting transfers between devices: none -> 10.3 us  [the longest x4 9.33 us: ring_work(): came = lax.ppermute(held, 'col', around)]
    ppermute x3, waiting for transfers between devices: 14.8 us -> 5.33 us  [all_sum(): keep = keep + lax.ppermute(keep, 'col', [(c, c ^ bit) for c in range(cols)])]
    ppermute x1, waiting for transfers between devices: 0.01 us -> 9.13 us  [all_sum(): keep = keep + lax.ppermute(keep, 'row', [(0, 1), (1, 0)])]
    pallas_call x3 -> x5, Pallas kernels: 26 us -> 32.5 us  [part_product(): pl.pallas_call(functools.partial(part_kernel, count, first), grid_spec=pl...]
    pallas_call x3 -> x1, Pallas kernels: 47.4 us -> 53.4 us  [part_update(): pl.pallas_call(functools.partial(part_update_kernel, count, first), grid_...]
  transfers between devices with their start and end apart: 49 -> 40, of which waited for: 19 -> 19; matrix products, arithmetic and copies ran while one was open for 4% -> 5% of each run, Pallas kernels for 24% -> 14%
where the time goes in v3:
time: 243 us; the launch traced here: 239 us
  Pallas kernels  96 us (40%)
  waiting for transfers between devices  81.3 us (33%)
  starting transfers between devices  45.8 us (19%)
  local copies, waits for them, and re-layouts  8.07 us (3%)
  other arithmetic  7.16 us (3%)
    pallas_call x1, Pallas kernels, part_update(): pl.pallas_call(functools.partial(part_update_kernel, count, first), grid_...  53.4 us
    pallas_call x5, Pallas kernels, part_product(): pl.pallas_call(functools.partial(part_kernel, count, first), grid_spec=pl...  32.5 us
    ppermute x2, waiting for transfers between devices, body(): got2 = lax.ppermute(lax.ppermute(halves[1], both, along), both, over)  23.1 us
    ppermute x4, waiting for transfers between devices, ring_work(): came = lax.ppermute(held, 'col', around)  17.5 us
    ppermute x2, waiting for transfers between devices, body(): lax.ppermute(give[p * b:(p + 1) * b], 'row', across)  11.4 us
    ppermute x4, starting transfers between devices, ring_work(): came = lax.ppermute(held, 'col', around)  9.33 us
    ppermute x1, waiting for transfers between devices, all_sum(): keep = keep + lax.ppermute(keep, 'row', [(0, 1), (1, 0)])  9.13 us
    ppermute x6, waiting for transfers between devices, ring_gather(): held = [lax.ppermute(block, 'col', around) for block in held]  6.6 us
  transfers between devices with their start and end apart: 40, of which 19 were waited for; matrix products, arithmetic and copies ran while one was open for 5% of the time, Pallas kernels for 14%

profile of v3, /device:TPU:0, one launch (start us, length us, event | category | flops | bytes accessed | tf_op | source)
XLA Modules:
  0.0 239.0 jit_solution(15069478194277037187)
XLA Ops:
  1.6 1.5 collective-permute-done
  3.3 3.0 %collective-permute-start.1 = (f32[1024,256]{1,0:T(8,128)S(1)}, f32[1024,256]{1,0:T(8,128)S(1)}, u32[]{:S(2)}, u32[]{:S(2)}) collective-permute-start(f32[1024,256]{1,0:T(8,128)S(1)} %pad_maximum_fusion.refs_0_), channel_id=1, source_target_pairs={{0,4},{1,3},{4,8},{5,1},{8,12},{9,5},{12,14},{13,9},{14,10},{15,13... | collective-permute-start | bytes 3145736 | tf_op jit(solution)/shard_map/ppermute | solution.py:319
  6.3 4.3 %part_product.5 = (f32[256,1024]{1,0:T(8,128)S(1)}, f32[8192,256]{1,0:T(8,128)}, f32[128,128]{1,0:T(8,128)S(1)}) custom-call(s32[1]{0:T(128)} %bitcast.19.index_ref, f32[8192,1024]{1,0:T(8,128)} %a_ref.11, f32[1024,256]{1,0:T(8,128)S(1)} %pad_maximum_fusion.refs_0_), custom_call_target="tpu_custom_call" | custom-call | flops 1610612736 | bytes 6291456 | tf_op jit(solution)/shard_map/part_product/pallas_call | solution.py:378
  10.6 8.5 %collective-permute-done.1.refs_0_ = f32[1024,256]{1,0:T(8,128)S(1)} collective-permute-done((f32[1024,256]{1,0:T(8,128)S(1)}, f32[1024,256]{1,0:T(8,128)S(1)}, u32[]{:S(2)}, u32[]{:S(2)}) %collective-permute-start.1) | collective-permute-done | bytes 1048608 | tf_op jit(solution)/shard_map/ppermute | solution.py:319
  19.2 2.1 collective-permute-start.2
  21.8 7.8 %part_product.6 = (f32[256,1024]{1,0:T(8,128)S(1)}, f32[8192,256]{1,0:T(8,128)}, f32[128,128]{1,0:T(8,128)S(1)}) custom-call(s32[2]{0:T(128)S(1)} %pad_add_fusion.index_ref, f32[8192,1024]{1,0:T(8,128)} %a_ref.11, f32[1024,256]{1,0:T(8,128)S(1)} %after.4.refs_0_, ...), custom_call_target="tpu_custom_call", output_to_operand_aliasing={{0}: (4, {}), {1}: (5, {})} | custom-call | flops 3221225472 | bytes 12582912 | tf_op jit(solution)/shard_map/part_product/pallas_call | solution.py:378
  29.6 4.6 %collective-permute-done.2.refs_0_ = f32[1024,256]{1,0:T(8,128)} collective-permute-done((f32[1024,256]{1,0:T(8,128)S(1)}, f32[1024,256]{1,0:T(8,128)}, u32[]{:S(2)}, u32[]{:S(2)}) %collective-permute-start.2) | collective-permute-done | bytes 1048608 | tf_op jit(solution)/shard_map/ppermute | solution.py:319
  34.2 1.3 after.5.refs_0_
  35.5 2.1 collective-permute-start.4
  38.2 7.8 %part_product.7 = (f32[256,1024]{1,0:T(8,128)S(1)}, f32[8192,256]{1,0:T(8,128)}, f32[128,128]{1,0:T(8,128)S(1)}) custom-call(s32[2]{0:T(128)S(1)} %pad_add_fusion.1.index_ref, f32[8192,1024]{1,0:T(8,128)} %a_ref.11, f32[1024,256]{1,0:T(8,128)S(1)} %after.5.refs_0_, ...), custom_call_target="tpu_custom_call", output_to_operand_aliasing={{0}: (4, {}), {1}: (5, {})} | custom-call | flops 3221225472 | bytes 12582912 | tf_op jit(solution)/shard_map/part_product/pallas_call | solution.py:378
  46.0 4.5 %collective-permute-done.4.refs_0_ = f32[1024,256]{1,0:T(8,128)} collective-permute-done((f32[1024,256]{1,0:T(8,128)S(1)}, f32[1024,256]{1,0:T(8,128)}, u32[]{:S(2)}, u32[]{:S(2)}) %collective-permute-start.4) | collective-permute-done | bytes 1048608 | tf_op jit(solution)/shard_map/ppermute | solution.py:319
  50.5 1.3 after.6.refs_0_
  52.7 2.1 collective-permute-start.6
  54.9 7.7 %part_product.8 = (f32[256,1024]{1,0:T(8,128)S(1)}, f32[8192,256]{1,0:T(8,128)}, f32[128,128]{1,0:T(8,128)S(1)}) custom-call(s32[2]{0:T(128)S(1)} %pad_add_fusion.2.index_ref, f32[8192,1024]{1,0:T(8,128)} %a_ref.11, f32[1024,256]{1,0:T(8,128)S(1)} %after.6.refs_0_, ...), custom_call_target="tpu_custom_call", output_to_operand_aliasing={{0}: (4, {}), {1}: (5, {})} | custom-call | flops 3221225472 | bytes 12582912 | tf_op jit(solution)/shard_map/part_product/pallas_call | solution.py:378
  62.6 1.1 after.7
  63.9 1.7 collective-permute-done.8
  65.8 5.0 %part_product.9 = (f32[256,1024]{1,0:T(8,128)S(1)}, f32[8192,256]{1,0:T(8,128)}, f32[128,128]{1,0:T(8,128)}) custom-call(s32[1]{0:T(128)} %bitcast.16.index_ref, f32[8192,1024]{1,0:T(8,128)} %a_ref.11, f32[1024,256]{1,0:T(8,128)S(1)} %pad_maximum_fusion.1.refs_0_, ...), custom_call_target="tpu_custom_call", output_to_operand_aliasing={{0}: (3, {}), {1}: (4, {})} | custom-call | flops 1610612736 | bytes 6291456 | tf_op jit(solution)/shard_map/part_product/pallas_call | solution.py:378
  71.1 1.7 collective-permute-start.11
  72.8 6.8 %collective-permute-done.11 = f32[128,512]{0,1:T(8,128)S(1)} collective-permute-done((f32[128,512]{0,1:T(8,128)S(1)}, f32[128,512]{0,1:T(8,128)S(1)}, u32[]{:S(2)}, u32[]{:S(2)}) %collective-permute-start.11) | collective-permute-done | bytes 262176 | tf_op jit(solution)/shard_map/ppermute | solution.py:521
  79.7 1.7 collective-permute-start.9
  81.3 1.3 collective-permute-start.12
  82.6 4.7 %collective-permute-done.9 = f32[128,512]{0,1:T(8,128)S(1)} collective-permute-done((f32[128,512]{0,1:T(8,128)S(1)}, f32[128,512]{0,1:T(8,128)S(1)}, u32[]{:S(2)}, u32[]{:S(2)}) %collective-permute-start.9) | collective-permute-done | bytes 262176 | tf_op jit(solution)/shard_map/ppermute | solution.py:521
  88.0 15.8 %collective-permute-done.12 = f32[512,128]{1,0:T(8,128)S(1)} collective-permute-done((f32[512,128]{1,0:T(8,128)S(1)}, f32[512,128]{1,0:T(8,128)S(1)}, u32[]{:S(2)}, u32[]{:S(2)}) %collective-permute-start.12) | collective-permute-done | bytes 262176 | tf_op jit(solution)/shard_map/ppermute | solution.py:532
  103.8 1.6 collective-permute-start.13
  105.6 7.3 %collective-permute-done.13 = f32[512,128]{1,0:T(8,128)S(1)} collective-permute-done((f32[512,128]{1,0:T(8,128)S(1)}, f32[512,128]{1,0:T(8,128)S(1)}, u32[]{:S(2)}, u32[]{:S(2)}) %collective-permute-start.13) | collective-permute-done | bytes 262176 | tf_op jit(solution)/shard_map/ppermute | solution.py:532
  112.9 1.9 own_gram.1
  115.1 1.9 collective-permute-start.14
  118.3 2.5 %collective-permute-start.20 = (f32[256,512]{0,1:T(8,128)}, f32[256,512]{0,1:T(8,128)}, u32[]{:S(2)}, u32[]{:S(2)}) collective-permute-start(f32[256,512]{0,1:T(8,128)} %pad_maximum_fusion.5), channel_id=1, source_target_pairs={{0,16},{16,0},{1,17},{17,1},{2,18},{18,2},{3,19},{19,3},{4,20},{20... | collective-permute-start | bytes 1572872 | tf_op jit(solution)/shard_map/ppermute | solution.py:548
  120.8 3.4 %collective-permute-done.24.refs_2_ = f32[1024,128]{1,0:T(8,128)S(1)} collective-permute-done((f32[1024,128]{1,0:T(8,128)S(1)}, f32[1024,128]{1,0:T(8,128)S(1)}, u32[]{:S(2)}, u32[]{:S(2)}) %collective-permute-start.24) | collective-permute-done | bytes 524320 | tf_op jit(solution)/shard_map/ppermute | solution.py:269
  124.2 2.5 %collective-permute-start.15 = (f32[128,256]{1,0:T(8,128)S(1)}, f32[128,256]{1,0:T(8,128)S(1)}, u32[]{:S(2)}, u32[]{:S(2)}) collective-permute-start(f32[128,256]{1,0:T(8,128)S(1)} %dynamic-slice_add_fusion.2), channel_id=1, source_target_pairs={{0,16},{16,0},{1,17},{17,1},{2,18},{18,2},{3,19},{19,3},{4,20},{20... | collective-permute-start | bytes 393224 | tf_op jit(solution)/shard_map/ppermute | solution.py:487
  126.8 9.1 %collective-permute-done.15 = f32[128,256]{1,0:T(8,128)S(1)} collective-permute-done((f32[128,256]{1,0:T(8,128)S(1)}, f32[128,256]{1,0:T(8,128)S(1)}, u32[]{:S(2)}, u32[]{:S(2)}) %collective-permute-start.15) | collective-permute-done | bytes 131104 | tf_op jit(solution)/shard_map/ppermute | solution.py:487
  135.9 1.7 collective-permute-start.16
  137.9 3.7 %collective-permute-done.16 = f32[128,256]{1,0:T(8,128)S(1)} collective-permute-done((f32[128,256]{1,0:T(8,128)S(1)}, f32[128,256]{1,0:T(8,128)S(1)}, u32[]{:S(2)}, u32[]{:S(2)}) %collective-permute-start.16) | collective-permute-done | bytes 131104 | tf_op jit(solution)/shard_map/ppermute | solution.py:490
  142.4 2.3 constant_dynamic-slice_fusion.2
  144.7 4.7 %collective-permute-start.21 = (f32[1024,256]{1,0:T(8,128)}, f32[1024,256]{1,0:T(8,128)}, u32[]{:S(2)}, u32[]{:S(2)}) collective-permute-start(f32[1024,256]{1,0:T(8,128)} %constant_dynamic-slice_fusion.2), channel_id=1, source_target_pairs={{0,16},{1,17},{2,18},{3,19},{4,20},{5,21},{6,22},{7,23},{24,8},{25... | collective-permute-start | bytes 3145736 | tf_op jit(solution)/shard_map/ppermute | solution.py:546
  149.5 3.4 %collective-permute-start.18 = (f32[128,256]{1,0:T(8,128)S(1)}, f32[128,256]{1,0:T(8,128)S(1)}, u32[]{:S(2)}, u32[]{:S(2)}) collective-permute-start(f32[128,256]{1,0:T(8,128)S(1)} %add.307), channel_id=1, source_target_pairs={{0,8},{1,9},{2,10},{3,11},{4,12},{5,13},{6,14},{7,15},{8,0},{9,1},... | collective-permute-start | bytes 393224 | tf_op jit(solution)/shard_map/ppermute | solution.py:490
  152.9 2.5 %collective-permute-start.32 = (f32[1024,128]{1,0:T(8,128)}, f32[1024,128]{1,0:T(8,128)S(1)}, u32[]{:S(2)}, u32[]{:S(2)}) collective-permute-start(f32[1024,128]{1,0:T(8,128)} %collective-permute-done.28.refs_6_), channel_id=1, source_target_pairs={{0,4},{1,3},{4,8},{5,1},{8,12},{9,5},{12,14},{13,9},{14,10},{15,13... | collective-permute-start | bytes 1572872 | tf_op jit(solution)/shard_map/ppermute | solution.py:269
  155.4 1.1 broadcast_select_fusion.2
  156.5 1.7 collective-permute-done.18
  158.3 1.7 collective-permute-start.33
  161.0 1.6 copy.14.zt_ref
  163.2 1.6 collective-permute-start.36
  164.8 3.2 %collective-permute-done.33.refs_11_ = f32[1024,128]{1,0:T(8,128)} collective-permute-done((f32[1024,128]{1,0:T(8,128)}, f32[1024,128]{1,0:T(8,128)}, u32[]{:S(2)}, u32[]{:S(2)}) %collective-permute-start.33) | collective-permute-done | bytes 524320 | tf_op jit(solution)/shard_map/ppermute | solution.py:269
  169.0 2.5 %collective-permute-start.38 = (f32[512,128]{1,0:T(8,128)S(1)}, f32[512,128]{1,0:T(8,128)S(1)}, u32[]{:S(2)}, u32[]{:S(2)}) collective-permute-start(f32[512,128]{1,0:T(8,128)S(1)} %constant_dynamic-slice_fusion), channel_id=1, source_target_pairs={{0,4},{1,3},{4,8},{5,1},{8,12},{9,5},{12,14},{13,9},{14,10},{15,13... | collective-permute-start | bytes 786440 | tf_op jit(solution)/shard_map/ppermute | solution.py:275
  171.5 1.4 broadcast_select_fusion
  173.0 2.4 %collective-permute-done.38 = f32[512,128]{1,0:T(8,128)S(1)} collective-permute-done((f32[512,128]{1,0:T(8,128)S(1)}, f32[512,128]{1,0:T(8,128)S(1)}, u32[]{:S(2)}, u32[]{:S(2)}) %collective-permute-start.38) | collective-permute-done | bytes 262176 | tf_op jit(solution)/shard_map/ppermute | solution.py:275
  175.5 4.4 %factors.1 = (bf16[512,1024]{1,0:T(8,128)(2,1)S(1)}, bf16[512,1024]{1,0:T(8,128)(2,1)S(1)}) custom-call(f32[2,128,128]{2,1,0:T(8,128)S(1)} %copy-done.4, f32[256,256]{1,0:T(8,128)S(1)} %pad_maximum_fusion.10.m_ref, f32[128,128]{1,0:T(8,128)S(1)} %slice.36.n_ref, f32[256,1024]{1,0:T(8,128)S(1)} %copy.14.zt_ref, f32[2,1024,128]{2,1,0:T(8,128)S(1)} %pad_maximum_fusion.3.vc_ref), custom_call_target="tpu_custom_call" | custom-call | tf_op jit(solution)/shard_map/factors/pallas_call | solution.py:153
  185.4 53.4 %part_update.1 = f32[8192,1024]{1,0:T(8,128)} custom-call(s32[16]{0:T(128)S(1)} %stack.109.index_ref, f32[8192,1024]{1,0:T(8,128)} %a_ref.11, f32[8192,256]{1,0:T(8,128)} %get-tuple-element.34.v_ref, bf16[512,1024]{1,0:T(8,128)(2,1)} %copy-done, bf16[512,1024]{1,0:T(8,128)(2,1)} %copy-done.1, f32[1024,128]{1,0:T(8,128)S(1)} %pad_maximum_fusion.6.refs_0_, ...), custom_call_target="tpu_custom_call" | custom-call | tf_op jit(solution)/shard_map/part_update/pallas_call | solution.py:464
  (102 shorter events, 16.8 us)
Async XLA Ops:
  1.1 2.1 collective-permute-start
  3.3 15.7 %collective-permute-start.1 = (f32[1024,256]{1,0:T(8,128)S(1)}, f32[1024,256]{1,0:T(8,128)S(1)}, u32[]{:S(2)}, u32[]{:S(2)}) collective-permute-start(f32[1024,256]{1,0:T(8,128)S(1)} %pad_maximum_fusion.refs_0_), channel_id=1, source_target_pairs={{0,4},{1,3},{4,8},{5,1},{8,12},{9,5},{12,14},{13,9},{14,10},{15,13... | collective-permute-start | bytes 3145736 | tf_op jit(solution)/shard_map/ppermute | solution.py:319
  19.1 2.7 %collective-permute-start.3 = (f32[1024,256]{1,0:T(8,128)S(1)}, f32[1024,256]{1,0:T(8,128)S(1)}, u32[]{:S(2)}, u32[]{:S(2)}) collective-permute-start(f32[1024,256]{1,0:T(8,128)S(1)} %after.4.refs_0_), channel_id=1, source_target_pairs={{0,1},{1,0},{2,3},{3,2},{4,5},{5,4},{6,7},{7,6},{8,9},{9,8},{10,11... | collective-permute-start | bytes 3145736 | tf_op jit(solution)/shard_map/ppermute | solution.py:322
  19.2 15.0 %collective-permute-start.2 = (f32[1024,256]{1,0:T(8,128)S(1)}, f32[1024,256]{1,0:T(8,128)}, u32[]{:S(2)}, u32[]{:S(2)}) collective-permute-start(f32[1024,256]{1,0:T(8,128)S(1)} %after.4.refs_0_), channel_id=1, source_target_pairs={{0,4},{1,3},{4,8},{5,1},{8,12},{9,5},{12,14},{13,9},{14,10},{15,13... | collective-permute-start | bytes 3145736 | tf_op jit(solution)/shard_map/ppermute | solution.py:319
  35.5 2.7 %collective-permute-start.5 = (f32[1024,256]{1,0:T(8,128)S(1)}, f32[1024,256]{1,0:T(8,128)S(1)}, u32[]{:S(2)}, u32[]{:S(2)}) collective-permute-start(f32[1024,256]{1,0:T(8,128)S(1)} %after.5.refs_0_), channel_id=1, source_target_pairs={{0,1},{1,0},{2,3},{3,2},{4,5},{5,4},{6,7},{7,6},{8,9},{9,8},{10,11... | collective-permute-start | bytes 3145736 | tf_op jit(solution)/shard_map/ppermute | solution.py:322
  35.5 15.0 %collective-permute-start.4 = (f32[1024,256]{1,0:T(8,128)S(1)}, f32[1024,256]{1,0:T(8,128)}, u32[]{:S(2)}, u32[]{:S(2)}) collective-permute-start(f32[1024,256]{1,0:T(8,128)S(1)} %after.5.refs_0_), channel_id=1, source_target_pairs={{0,4},{1,3},{4,8},{5,1},{8,12},{9,5},{12,14},{13,9},{14,10},{15,13... | collective-permute-start | bytes 3145736 | tf_op jit(solution)/shard_map/ppermute | solution.py:319
  51.8 3.1 %collective-permute-start.7 = (f32[1024,256]{1,0:T(8,128)S(1)}, f32[1024,256]{1,0:T(8,128)S(1)}, u32[]{:S(2)}, u32[]{:S(2)}) collective-permute-start(f32[1024,256]{1,0:T(8,128)S(1)} %after.6.refs_0_), channel_id=1, source_target_pairs={{0,1},{1,0},{2,3},{3,2},{4,5},{5,4},{6,7},{7,6},{8,9},{9,8},{10,11... | collective-permute-start | bytes 3145736 | tf_op jit(solution)/shard_map/ppermute | solution.py:322
  52.7 9.9 %collective-permute-start.6 = (f32[512,256]{1,0:T(8,128)}, f32[512,256]{1,0:T(8,128)}, u32[]{:S(2)}, u32[]{:S(2)}) collective-permute-start(f32[512,256]{1,0:T(8,128)} %constant_dynamic-slice_fusion.5), channel_id=1, source_target_pairs={{0,4},{1,3},{4,8},{5,1},{8,12},{9,5},{12,14},{13,9},{14,10},{15,13... | collective-permute-start | bytes 1572872 | tf_op jit(solution)/shard_map/ppermute | solution.py:319
  63.7 2.0 collective-permute-start.8
  71.1 8.5 %collective-permute-start.11 = (f32[128,512]{0,1:T(8,128)S(1)}, f32[128,512]{0,1:T(8,128)S(1)}, u32[]{:S(2)}, u32[]{:S(2)}) collective-permute-start(f32[128,512]{0,1:T(8,128)S(1)} %dynamic-slice.3), channel_id=1, source_target_pairs={{0,16},{16,0},{1,17},{17,1},{2,18},{18,2},{3,19},{19,3},{4,20},{20... | collective-permute-start | bytes 786440 | tf_op jit(solution)/shard_map/ppermute | solution.py:521
  79.7 7.6 %collective-permute-start.9 = (f32[128,512]{0,1:T(8,128)S(1)}, f32[128,512]{0,1:T(8,128)S(1)}, u32[]{:S(2)}, u32[]{:S(2)}) collective-permute-start(f32[128,512]{0,1:T(8,128)S(1)} %get-tuple-element.44), channel_id=1, source_target_pairs={{0,16},{16,0},{1,17},{17,1},{2,18},{18,2},{3,19},{19,3},{4,20},{20... | collective-permute-start | bytes 786440 | tf_op jit(solution)/shard_map/ppermute | solution.py:521
  81.3 22.5 %collective-permute-start.12 = (f32[512,128]{1,0:T(8,128)S(1)}, f32[512,128]{1,0:T(8,128)S(1)}, u32[]{:S(2)}, u32[]{:S(2)}) collective-permute-start(f32[512,128]{1,0:T(8,128)S(1)} %bitcast.37), channel_id=1, source_target_pairs={{8,0},{9,1},{10,2},{11,3},{12,4},{13,5},{14,6},{15,7},{16,24},{17,... | collective-permute-start | bytes 786440 | tf_op jit(solution)/shard_map/ppermute | solution.py:532
  87.3 18.1 %collective-permute-start.10 = (f32[512,128]{1,0:T(8,128)S(1)}, f32[512,128]{1,0:T(8,128)S(1)}, u32[]{:S(2)}, u32[]{:S(2)}) collective-permute-start(f32[512,128]{1,0:T(8,128)S(1)} %bitcast.38), channel_id=1, source_target_pairs={{8,16},{9,17},{10,18},{11,19},{12,20},{13,21},{14,22},{15,23},{16,... | collective-permute-start | bytes 786440 | tf_op jit(solution)/shard_map/ppermute | solution.py:531
  103.8 9.0 %collective-permute-start.13 = (f32[512,128]{1,0:T(8,128)S(1)}, f32[512,128]{1,0:T(8,128)S(1)}, u32[]{:S(2)}, u32[]{:S(2)}) collective-permute-start(f32[512,128]{1,0:T(8,128)S(1)} %collective-permute-done.12), channel_id=1, source_target_pairs={{0,16},{1,17},{2,18},{3,19},{4,20},{5,21},{6,22},{7,23},{24,8},{25... | collective-permute-start | bytes 786440 | tf_op jit(solution)/shard_map/ppermute | solution.py:532
  105.4 9.4 %collective-permute-start.22 = (f32[512,128]{1,0:T(8,128)S(1)}, f32[512,128]{1,0:T(8,128)S(1)}, u32[]{:S(2)}, u32[]{:S(2)}) collective-permute-start(f32[512,128]{1,0:T(8,128)S(1)} %broadcast_select_fusion.16.z1_ref), channel_id=1, source_target_pairs={{0,1},{1,0},{2,3},{3,2},{4,5},{5,4},{6,7},{7,6},{8,9},{9,8},{10,11... | collective-permute-start | bytes 786440 | tf_op jit(solution)/shard_map/ppermute | solution.py:262
  112.9 4.1 %collective-permute-start.23 = (f32[512,128]{1,0:T(8,128)S(1)}, f32[512,128]{1,0:T(8,128)S(1)}, u32[]{:S(2)}, u32[]{:S(2)}) collective-permute-start(f32[512,128]{1,0:T(8,128)S(1)} %broadcast_select_fusion.15.z2_ref), channel_id=1, source_target_pairs={{0,1},{1,0},{2,3},{3,2},{4,5},{5,4},{6,7},{7,6},{8,9},{9,8},{10,11... | collective-permute-start | bytes 786440 | tf_op jit(solution)/shard_map/ppermute | solution.py:262
  115.0 9.2 %collective-permute-start.24 = (f32[1024,128]{1,0:T(8,128)S(1)}, f32[1024,128]{1,0:T(8,128)S(1)}, u32[]{:S(2)}, u32[]{:S(2)}) collective-permute-start(f32[1024,128]{1,0:T(8,128)S(1)} %pad_maximum_fusion.6.refs_0_), channel_id=1, source_target_pairs={{0,4},{1,3},{4,8},{5,1},{8,12},{9,5},{12,14},{13,9},{14,10},{15,13... | collective-permute-start | bytes 1572872 | tf_op jit(solution)/shard_map/ppermute | solution.py:269
  115.1 9.2 %collective-permute-start.14 = (f32[128,256]{1,0:T(8,128)S(1)}, f32[128,256]{1,0:T(8,128)S(1)}, u32[]{:S(2)}, u32[]{:S(2)}) collective-permute-start(f32[128,256]{1,0:T(8,128)S(1)} %constant_dynamic-slice_fusion.3), channel_id=1, source_target_pairs={{0,1},{1,0},{2,3},{3,2},{4,5},{5,4},{6,7},{7,6},{8,9},{9,8},{10,11... | collective-permute-start | bytes 393224 | tf_op jit(solution)/shard_map/ppermute | solution.py:486
  117.0 20.6 %collective-permute-start.25 = (f32[1024,128]{1,0:T(8,128)S(1)}, f32[1024,128]{1,0:T(8,128)S(1)}, u32[]{:S(2)}, u32[]{:S(2)}) collective-permute-start(f32[1024,128]{1,0:T(8,128)S(1)} %pad_maximum_fusion.7.refs_1_), channel_id=1, source_target_pairs={{0,4},{1,3},{4,8},{5,1},{8,12},{9,5},{12,14},{13,9},{14,10},{15,13... | collective-permute-start | bytes 1572872 | tf_op jit(solution)/shard_map/ppermute | solution.py:269
  118.3 37.1 %collective-permute-start.20 = (f32[256,512]{0,1:T(8,128)}, f32[256,512]{0,1:T(8,128)}, u32[]{:S(2)}, u32[]{:S(2)}) collective-permute-start(f32[256,512]{0,1:T(8,128)} %pad_maximum_fusion.5), channel_id=1, source_target_pairs={{0,16},{16,0},{1,17},{17,1},{2,18},{18,2},{3,19},{19,3},{4,20},{20... | collective-permute-start | bytes 1572872 | tf_op jit(solution)/shard_map/ppermute | solution.py:548
  124.2 28.7 %collective-permute-start.28 = (f32[1024,128]{1,0:T(8,128)S(1)}, f32[1024,128]{1,0:T(8,128)}, u32[]{:S(2)}, u32[]{:S(2)}) collective-permute-start(f32[1024,128]{1,0:T(8,128)S(1)} %collective-permute-done.24.refs_2_), channel_id=1, source_target_pairs={{0,4},{1,3},{4,8},{5,1},{8,12},{9,5},{12,14},{13,9},{14,10},{15,13... | collective-permute-start | bytes 1572872 | tf_op jit(solution)/shard_map/ppermute | solution.py:269
  124.2 11.7 %collective-permute-start.15 = (f32[128,256]{1,0:T(8,128)S(1)}, f32[128,256]{1,0:T(8,128)S(1)}, u32[]{:S(2)}, u32[]{:S(2)}) collective-permute-start(f32[128,256]{1,0:T(8,128)S(1)} %dynamic-slice_add_fusion.2), channel_id=1, source_target_pairs={{0,16},{16,0},{1,17},{17,1},{2,18},{18,2},{3,19},{19,3},{4,20},{20... | collective-permute-start | bytes 393224 | tf_op jit(solution)/shard_map/ppermute | solution.py:487
  135.9 5.6 %collective-permute-start.16 = (f32[128,256]{1,0:T(8,128)S(1)}, f32[128,256]{1,0:T(8,128)S(1)}, u32[]{:S(2)}, u32[]{:S(2)}) collective-permute-start(f32[128,256]{1,0:T(8,128)S(1)} %add.305), channel_id=1, source_target_pairs={{0,2},{1,3},{2,0},{3,1},{4,6},{5,7},{6,4},{7,5},{8,10},{9,11},{10,... | collective-permute-start | bytes 393224 | tf_op jit(solution)/shard_map/ppermute | solution.py:490
  137.6 22.3 %copy-start.2 = (f32[1024,128]{1,0:T(8,128)}, f32[1024,128]{1,0:T(8,128)S(1)}, u32[]{:S(2)}) copy-start(f32[1024,128]{1,0:T(8,128)S(1)} %collective-permute-done.25.refs_3_) | copy-start | bytes 1572868
  137.6 20.7 %collective-permute-start.29 = (f32[1024,128]{1,0:T(8,128)S(1)}, f32[1024,128]{1,0:T(8,128)}, u32[]{:S(2)}, u32[]{:S(2)}) collective-permute-start(f32[1024,128]{1,0:T(8,128)S(1)} %collective-permute-done.25.refs_3_), channel_id=1, source_target_pairs={{0,4},{1,3},{4,8},{5,1},{8,12},{9,5},{12,14},{13,9},{14,10},{15,13... | collective-permute-start | bytes 1572872 | tf_op jit(solution)/shard_map/ppermute | solution.py:269
  141.6 7.9 %collective-permute-start.17 = (f32[128,256]{1,0:T(8,128)S(1)}, f32[128,256]{1,0:T(8,128)S(1)}, u32[]{:S(2)}, u32[]{:S(2)}) collective-permute-start(f32[128,256]{1,0:T(8,128)S(1)} %add.306), channel_id=1, source_target_pairs={{0,4},{1,5},{2,6},{3,7},{4,0},{5,1},{6,2},{7,3},{8,12},{9,13},{10,... | collective-permute-start | bytes 393224 | tf_op jit(solution)/shard_map/ppermute | solution.py:490
  144.7 26.8 %collective-permute-start.21 = (f32[1024,256]{1,0:T(8,128)}, f32[1024,256]{1,0:T(8,128)}, u32[]{:S(2)}, u32[]{:S(2)}) collective-permute-start(f32[1024,256]{1,0:T(8,128)} %constant_dynamic-slice_fusion.2), channel_id=1, source_target_pairs={{0,16},{1,17},{2,18},{3,19},{4,20},{5,21},{6,22},{7,23},{24,8},{25... | collective-permute-start | bytes 3145736 | tf_op jit(solution)/shard_map/ppermute | solution.py:546
  149.4 26.2 %copy-start.4 = (f32[2,128,128]{2,1,0:T(8,128)S(1)}, f32[2,128,128]{2,1,0:T(8,128)}, u32[]{:S(2)}) copy-start(f32[2,128,128]{2,1,0:T(8,128)} %t_ref.1) | copy-start | bytes 393220
  149.5 8.7 %collective-permute-start.18 = (f32[128,256]{1,0:T(8,128)S(1)}, f32[128,256]{1,0:T(8,128)S(1)}, u32[]{:S(2)}, u32[]{:S(2)}) collective-permute-start(f32[128,256]{1,0:T(8,128)S(1)} %add.307), channel_id=1, source_target_pairs={{0,8},{1,9},{2,10},{3,11},{4,12},{5,13},{6,14},{7,15},{8,0},{9,1},... | collective-permute-start | bytes 393224 | tf_op jit(solution)/shard_map/ppermute | solution.py:490
  152.9 10.3 %collective-permute-start.32 = (f32[1024,128]{1,0:T(8,128)}, f32[1024,128]{1,0:T(8,128)S(1)}, u32[]{:S(2)}, u32[]{:S(2)}) collective-permute-start(f32[1024,128]{1,0:T(8,128)} %collective-permute-done.28.refs_6_), channel_id=1, source_target_pairs={{0,4},{1,3},{4,8},{5,1},{8,12},{9,5},{12,14},{13,9},{14,10},{15,13... | collective-permute-start | bytes 1572872 | tf_op jit(solution)/shard_map/ppermute | solution.py:269
  158.2 4.4 %collective-permute-start.19 = (f32[128,256]{1,0:T(8,128)S(1)}, f32[128,256]{1,0:T(8,128)S(1)}, u32[]{:S(2)}, u32[]{:S(2)}) collective-permute-start(f32[128,256]{1,0:T(8,128)S(1)} %add.308), channel_id=1, source_target_pairs={{0,1},{1,0},{2,3},{3,2},{4,5},{5,4},{6,7},{7,6},{8,9},{9,8},{10,11... | collective-permute-start | bytes 393224 | tf_op jit(solution)/shard_map/ppermute | solution.py:492
  158.3 9.7 %collective-permute-start.33 = (f32[1024,128]{1,0:T(8,128)}, f32[1024,128]{1,0:T(8,128)}, u32[]{:S(2)}, u32[]{:S(2)}) collective-permute-start(f32[1024,128]{1,0:T(8,128)} %collective-permute-done.29.refs_7_), channel_id=1, source_target_pairs={{0,4},{1,3},{4,8},{5,1},{8,12},{9,5},{12,14},{13,9},{14,10},{15,13... | collective-permute-start | bytes 1572872 | tf_op jit(solution)/shard_map/ppermute | solution.py:269
  162.5 22.9 %copy-start.3 = (f32[1024,128]{1,0:T(8,128)S(1)}, f32[1024,128]{1,0:T(8,128)}, u32[]{:S(2)}) copy-start(f32[1024,128]{1,0:T(8,128)} %copy-done.2) | copy-start | bytes 1572868
  162.6 18.0 %collective-permute-start.26 = (f32[1024,128]{1,0:T(8,128)S(1)}, f32[1024,128]{1,0:T(8,128)S(1)}, u32[]{:S(2)}, u32[]{:S(2)}) collective-permute-start(f32[1024,128]{1,0:T(8,128)S(1)} %collective-permute-done.24.refs_2_), channel_id=1, source_target_pairs={{0,1},{1,0},{2,3},{3,2},{4,5},{5,4},{6,7},{7,6},{8,9},{9,8},{10,11... | collective-permute-start | bytes 1572872 | tf_op jit(solution)/shard_map/ppermute | solution.py:271
  162.7 20.3 %collective-permute-start.27 = (f32[1024,128]{1,0:T(8,128)}, f32[1024,128]{1,0:T(8,128)S(1)}, u32[]{:S(2)}, u32[]{:S(2)}) collective-permute-start(f32[1024,128]{1,0:T(8,128)} %copy-done.2), channel_id=1, source_target_pairs={{0,1},{1,0},{2,3},{3,2},{4,5},{5,4},{6,7},{7,6},{8,9},{9,8},{10,11... | collective-permute-start | bytes 1572872 | tf_op jit(solution)/shard_map/ppermute | solution.py:271
  163.2 9.6 %collective-permute-start.36 = (f32[512,128]{1,0:T(8,128)S(1)}, f32[512,128]{1,0:T(8,128)S(1)}, u32[]{:S(2)}, u32[]{:S(2)}) collective-permute-start(f32[512,128]{1,0:T(8,128)S(1)} %constant_dynamic-slice_fusion.1), channel_id=1, source_target_pairs={{0,4},{1,3},{4,8},{5,1},{8,12},{9,5},{12,14},{13,9},{14,10},{15,13... | collective-permute-start | bytes 786440 | tf_op jit(solution)/shard_map/ppermute | solution.py:275
  169.0 6.4 %collective-permute-start.38 = (f32[512,128]{1,0:T(8,128)S(1)}, f32[512,128]{1,0:T(8,128)S(1)}, u32[]{:S(2)}, u32[]{:S(2)}) collective-permute-start(f32[512,128]{1,0:T(8,128)S(1)} %constant_dynamic-slice_fusion), channel_id=1, source_target_pairs={{0,4},{1,3},{4,8},{5,1},{8,12},{9,5},{12,14},{13,9},{14,10},{15,13... | collective-permute-start | bytes 786440 | tf_op jit(solution)/shard_map/ppermute | solution.py:275
  172.9 7.8 %collective-permute-start.37 = (f32[512,128]{1,0:T(8,128)S(1)}, f32[512,128]{1,0:T(8,128)S(1)}, u32[]{:S(2)}, u32[]{:S(2)}) collective-permute-start(f32[512,128]{1,0:T(8,128)S(1)} %collective-permute-done.36), channel_id=1, source_target_pairs={{0,1},{1,0},{2,3},{3,2},{4,5},{5,4},{6,7},{7,6},{8,9},{9,8},{10,11... | collective-permute-start | bytes 786440 | tf_op jit(solution)/shard_map/ppermute | solution.py:262
  175.4 5.7 %collective-permute-start.39 = (f32[512,128]{1,0:T(8,128)S(1)}, f32[512,128]{1,0:T(8,128)S(1)}, u32[]{:S(2)}, u32[]{:S(2)}) collective-permute-start(f32[512,128]{1,0:T(8,128)S(1)} %collective-permute-done.38), channel_id=1, source_target_pairs={{0,1},{1,0},{2,3},{3,2},{4,5},{5,4},{6,7},{7,6},{8,9},{9,8},{10,11... | collective-permute-start | bytes 786440 | tf_op jit(solution)/shard_map/ppermute | solution.py:262
  180.0 3.8 %copy-start = (bf16[512,1024]{1,0:T(8,128)(2,1)}, bf16[512,1024]{1,0:T(8,128)(2,1)S(1)}, u32[]{:S(2)}) copy-start(bf16[512,1024]{1,0:T(8,128)(2,1)S(1)} %get-tuple-element.37.hi_ref) | copy-start | bytes 3145732
  180.0 4.6 %copy-start.1 = (bf16[512,1024]{1,0:T(8,128)(2,1)}, bf16[512,1024]{1,0:T(8,128)(2,1)S(1)}, u32[]{:S(2)}) copy-start(bf16[512,1024]{1,0:T(8,128)(2,1)S(1)} %get-tuple-element.38.lo_ref) | copy-start | bytes 3145732
  180.0 3.0 %collective-permute-start.30 = (f32[1024,128]{1,0:T(8,128)}, f32[1024,128]{1,0:T(8,128)S(1)}, u32[]{:S(2)}, u32[]{:S(2)}) collective-permute-start(f32[1024,128]{1,0:T(8,128)} %collective-permute-done.28.refs_6_), channel_id=1, source_target_pairs={{0,1},{1,0},{2,3},{3,2},{4,5},{5,4},{6,7},{7,6},{8,9},{9,8},{10,11... | collective-permute-start | bytes 1572872 | tf_op jit(solution)/shard_map/ppermute | solution.py:271
  180.6 3.2 %collective-permute-start.31 = (f32[1024,128]{1,0:T(8,128)}, f32[1024,128]{1,0:T(8,128)S(1)}, u32[]{:S(2)}, u32[]{:S(2)}) collective-permute-start(f32[1024,128]{1,0:T(8,128)} %collective-permute-done.29.refs_7_), channel_id=1, source_target_pairs={{0,1},{1,0},{2,3},{3,2},{4,5},{5,4},{6,7},{7,6},{8,9},{9,8},{10,11... | collective-permute-start | bytes 1572872 | tf_op jit(solution)/shard_map/ppermute | solution.py:271
  180.7 3.2 %collective-permute-start.34 = (f32[1024,128]{1,0:T(8,128)S(1)}, f32[1024,128]{1,0:T(8,128)S(1)}, u32[]{:S(2)}, u32[]{:S(2)}) collective-permute-start(f32[1024,128]{1,0:T(8,128)S(1)} %collective-permute-done.32.refs_10_), channel_id=1, source_target_pairs={{0,1},{1,0},{2,3},{3,2},{4,5},{5,4},{6,7},{7,6},{8,9},{9,8},{10,11... | collective-permute-start | bytes 1572872 | tf_op jit(solution)/shard_map/ppermute | solution.py:271
  181.1 3.5 %collective-permute-start.35 = (f32[1024,128]{1,0:T(8,128)}, f32[1024,128]{1,0:T(8,128)S(1)}, u32[]{:S(2)}, u32[]{:S(2)}) collective-permute-start(f32[1024,128]{1,0:T(8,128)} %collective-permute-done.33.refs_11_), channel_id=1, source_target_pairs={{0,1},{1,0},{2,3},{3,2},{4,5},{5,4},{6,7},{7,6},{8,9},{9,8},{10,11... | collective-permute-start | bytes 1572872 | tf_op jit(solution)/shard_map/ppermute | solution.py:271
  183.8 0.8 copy-start.5
  184.6 0.8 copy-start.6
